TPU v7x, 256 devices: a whole 4x4x8 slice. The times are simulated.
256 devices in a mesh: dp: 64 (over x, y_hi, z), ctx: 4 (over y_lo, core).
Axes of the slice: x: 4, y: 4 (y_hi: 2, y_lo: 2; y = y_hi * 2 + y_lo), z: 8, core: 2. Of those that a mesh axis runs over, the one named last changes fastest.
Arguments:
- frames: bfloat16 [64, 1024, 1536], P('dp', 'ctx'), may hold values from -6 to 6
- destinations: int32 [64, 1024], P('dp', 'ctx'), may hold values from 0 to 16383, as said below
- segments: int32 [64, 1024], P('dp'), may hold values from 0 to 2, as said below
- tile_mask: int32 [64, 8, 8], P('dp', 'ctx'), may hold values from 0 to 1, as said below
- attn_gain: float32 [1536], replicated, may hold values from 0.1 to 1.9
- w_qkv: bfloat16 [1536, 2304], replicated
- w_out: bfloat16 [768, 1536], replicated, may hold values from -5 to 5
- conv_gain: float32 [1536], replicated, may hold values from 0.1 to 1.9
- w_pointin: bfloat16 [1536, 1536], P(('dp', 'ctx')), may hold values from -0.625 to 0.625
- w_pointout: bfloat16 [768, 1536], P(None, ('dp', 'ctx')), may hold values from -0.43164062 to 0.43164062
- w_depth: float32 [32, 768], replicated, may hold values from -1 to 1
- bn_scale: float32 [768], replicated, may hold values from 0.1 to 1.9
- bn_shift: float32 [768], replicated, may hold values from -3 to 3
Outputs:
- layer_out: bfloat16 [64, 1024, 1536], P('dp', 'ctx')
Inputs may be any that keep to these rules, and one draw needn't show every extreme that they name: `destinations`: per ctx index c, the values at positions c * 256 to (c + 1) * 256 - 1 over all rows of the first dimension are all different, so every target row is filled once. The rows of one device send at most 8 frames to one sequence, and exactly 8 to some sequences. `segments`: along a sequence the ids never fall, start at 0 and end at 2. tile_mask[b, t, t] = 1; tile_mask[b, t, u] = 0 where tiles t and u of sequence b share no segment id.
All inputs are finite; a program needn't handle non-finite values.
Results may differ from a plain program's by a relative error of at most 0.01.
Values may be sent and summed in bfloat16 or wider, within the bound.
A program may use at most 128 MiB of HBM per device.

v0:
```python
import math

import jax
import jax.numpy as jnp
from jax import lax
from jax.sharding import PartitionSpec as P

HEADS = 8


def padded_2(cells, sides, width):
    for axis, dim in sides:
        count = lax.axis_size(axis)
        ends = count - 1
        head = lax.slice_in_dim(cells, 0, width, axis=dim)
        tail = lax.slice_in_dim(cells, cells.shape[dim] - width, cells.shape[dim], axis=dim)
        cells = jnp.concatenate(
            [
                lax.ppermute(tail, axis, [(i, (i + 1) % count) for i in range(ends)]),
                cells,
                lax.ppermute(head, axis, [((i + 1) % count, i) for i in range(ends)]),
            ],
            axis=dim,
        )
    return cells


def layer_norm(values, gain):
    as_float = values.astype(jnp.float32)
    row_mean = jnp.mean(as_float, axis=-1, keepdims=True)
    centred = as_float - row_mean
    row_var = jnp.mean(centred * centred, axis=-1, keepdims=True)
    return centred * lax.rsqrt(row_var + 1e-06) * gain


def per_device(
    frames,
    destinations,
    segments,
    tile_mask,
    attn_gain,
    w_qkv,
    w_out,
    conv_gain,
    w_pointin,
    w_pointout,
    w_depth,
    bn_scale,
    bn_shift,
):
    row_count = frames.shape[1]
    width = frames.shape[2]
    peer_count = lax.axis_size("dp")
    capacity = 2 * row_count // peer_count
    own_frames = frames[0]
    targets = destinations[0]
    owner_index = targets // row_count
    slot_index = targets % row_count
    onehot = (owner_index[:, None] == jnp.arange(peer_count, dtype=jnp.int32)[None, :]).astype(
        jnp.int32
    )
    before = jnp.cumsum(onehot, axis=0) - onehot
    rank_in = jnp.sum(before * onehot, axis=1)
    position = owner_index * capacity + rank_in
    send_rows = jnp.zeros((peer_count * capacity, width), jnp.bfloat16).at[position].set(own_frames)
    send_slots = (
        jnp.full((peer_count * capacity,), row_count, jnp.int32).at[position].set(slot_index)
    )
    got_rows, got_slots = (
        lax.all_to_all(
            send_rows.reshape(peer_count, capacity, width),
            "dp",
            split_axis=0,
            concat_axis=0,
            tiled=True,
        ),
        lax.all_to_all(
            send_slots.reshape(peer_count, capacity), "dp", split_axis=0, concat_axis=0, tiled=True
        ),
    )
    placed = (
        jnp.zeros((row_count, width), jnp.bfloat16)
        .at[got_slots.reshape(-1)]
        .set(got_rows.reshape(-1, width), mode="drop")
    )
    shard_start = lax.axis_index("ctx") * row_count
    seg_row = segments[0]
    own_seg = lax.dynamic_slice_in_dim(seg_row, shard_start, row_count, 0)
    mask_rows = tile_mask[0]
    tile_size = row_count // mask_rows.shape[0]
    head_cols = w_out.shape[0]
    head_size = head_cols // HEADS
    scale_factor = 1.0 / math.sqrt(head_size)
    normed = layer_norm(placed, attn_gain).astype(jnp.bfloat16)
    qkv_rows = jnp.dot(normed, w_qkv, preferred_element_type=jnp.float32).astype(jnp.bfloat16)
    queries = qkv_rows[:, :head_cols].reshape(row_count, HEADS, head_size)
    key_rows = qkv_rows[:, head_cols : 2 * head_cols].reshape(row_count, HEADS, head_size)
    value_rows = qkv_rows[:, 2 * head_cols :].reshape(row_count, HEADS, head_size)

    def absorb(carry, block):
        key_block, value_block, seg_block, mask_block = block
        wide_mask = jnp.repeat(jnp.repeat(mask_block, tile_size, axis=0), tile_size, axis=1)
        allowed = (own_seg[:, None] == seg_block[None, :]) & (wide_mask == 1)
        running_max, running_sum, weighted = carry
        scores = (
            jnp.einsum("qhd,khd->hqk", queries, key_block, preferred_element_type=jnp.float32)
            * scale_factor
        )
        scores = jnp.where(allowed[None], scores, -1e30)
        new_max = jnp.maximum(running_max, jnp.max(scores, axis=-1))
        weights = jnp.where(allowed[None], jnp.exp(scores - new_max[:, :, None]), 0.0)
        factor = jnp.exp(running_max - new_max)
        new_sum = running_sum * factor + jnp.sum(weights, axis=-1)
        product = jnp.einsum(
            "hqk,khd->hqd",
            weights.astype(jnp.bfloat16),
            value_block,
            preferred_element_type=jnp.float32,
        )
        return ((new_max, new_sum, weighted * factor[:, :, None] + product), None)

    start_state = (
        jnp.full((HEADS, row_count), -1e30, jnp.float32),
        jnp.zeros((HEADS, row_count), jnp.float32),
        jnp.zeros((HEADS, row_count, head_size), jnp.float32),
    )
    keys_piece = lax.all_gather(key_rows, "ctx", axis=0, tiled=True)
    values_piece = lax.all_gather(value_rows, "ctx", axis=0, tiled=True)
    count = keys_piece.shape[0]
    block_rows = math.gcd(count, 512)
    blocks = count // block_rows
    mask_piece = mask_rows
    mask_piece = jnp.transpose(
        mask_piece.reshape(mask_rows.shape[0], blocks, block_rows // tile_size), (1, 0, 2)
    )
    inputs = (
        keys_piece.reshape(blocks, block_rows, HEADS, head_size),
        values_piece.reshape(blocks, block_rows, HEADS, head_size),
        seg_row.reshape(blocks, block_rows),
        mask_piece,
    )
    result, unused = lax.scan(absorb, start_state, inputs)
    final_max, final_sum, weighted = result
    attended = (
        jnp.transpose(weighted / final_sum[:, :, None], (1, 0, 2))
        .reshape(row_count, head_cols)
        .astype(jnp.bfloat16)
    )
    branch = jnp.dot(attended, w_out, preferred_element_type=jnp.float32)
    after_attn = (placed.astype(jnp.float32) + branch).astype(jnp.bfloat16)
    conv_normed = layer_norm(after_attn, conv_gain).astype(jnp.bfloat16)
    channels = w_depth.shape[1]
    projected = jnp.dot(
        conv_normed,
        lax.all_gather(w_pointin, ("dp", "ctx"), axis=0, tiled=True),
        preferred_element_type=jnp.float32,
    )
    gated = (projected[:, :channels] * jax.nn.sigmoid(projected[:, channels:])).astype(jnp.bfloat16)
    kernel_len = w_depth.shape[0]
    half_len = kernel_len // 2
    padded = padded_2(gated, (("ctx", 0),), half_len)
    padded_f = padded.astype(jnp.float32)
    seg_pad = jnp.pad(seg_row, (half_len, half_len), constant_values=-1)
    seg_near = lax.dynamic_slice_in_dim(seg_pad, shard_start, row_count + 2 * half_len, 0)
    depthwise = jnp.zeros((row_count, channels), jnp.float32)
    for tap_index in range(kernel_len):
        same_seg = (seg_near[tap_index : tap_index + row_count] == own_seg).astype(jnp.float32)
        depthwise = (
            depthwise
            + w_depth[tap_index][None, :]
            * padded_f[tap_index : tap_index + row_count]
            * same_seg[:, None]
        )
    shifted = depthwise * bn_scale + bn_shift
    activated = (shifted * jax.nn.sigmoid(shifted)).astype(jnp.bfloat16)
    closing = jnp.dot(
        activated,
        lax.all_gather(w_pointout, ("dp", "ctx"), axis=1, tiled=True),
        preferred_element_type=jnp.float32,
    )
    layer_out = (after_attn.astype(jnp.float32) + closing).astype(jnp.bfloat16)
    return layer_out[None]


def solution(mesh):
    return jax.shard_map(
        per_device,
        mesh=mesh,
        in_specs=(
            P("dp", "ctx", None),
            P("dp", "ctx"),
            P("dp", None),
            P("dp", "ctx", None),
            P(),
            P(),
            P(),
            P(),
            P(("dp", "ctx"), None),
            P(None, ("dp", "ctx")),
            P(),
            P(),
            P(),
        ),
        out_specs=P("dp", "ctx", None),
        check_vma=False,
    )
```

profile of v0, /device:TPU:1, one launch (start us, length us, event | category | flops | bytes accessed | tf_op | source)
XLA Modules:
  0.0 1003.2 jit_solution(10388988709967639840)
XLA Ops:
  6.5 0.8 and_select_fusion.2
  7.4 0.6 reduce-window.6
  8.0 0.2 slice_reduce_fusion
  8.2 0.7 and_select_fusion.1
  8.9 0.1 fusion.115
  9.0 0.7 compare_select_fusion.1
  9.7 1.4 scatter_custom_fusion
  11.1 0.7 all_to_all.9
  11.8 15.1 %all-to-all-start = ((s32[64,1,8]{2,1,0:T(1,128)}), s32[64,1,8]{2,1,0:T(1,128)S(1)}, u32[]{:S(2)}, u32[]{:S(2)}) async-start(s32[64,1,8]{2,1,0:T(1,128)} %bitcast.6), calls=%async_computation | async-start | bytes 65536 | tf_op jit(solution)/shard_map/all_to_all | solution.py:77
  26.9 3.7 scatter_custom_fusion.1
  30.7 6.9 all-to-all-done
  37.6 5.5 all-to-all-start.1
  43.2 0.6 broadcast.383
  43.8 0.8 reduce.73
  44.6 0.1 reshape.284
  44.7 35.7 %all-to-all-done.1 = bf16[64,8,1536]{2,1,0:T(8,128)(2,1)} async-done(((bf16[64,8,1536]{2,1,0:T(8,128)(2,1)}), bf16[64,8,1536]{2,1,0:T(8,128)(2,1)}, u32[]{:S(2)}, u32[]{:S(2)}) %all-to-all-start.1) | async-done | bytes 1572896 | tf_op jit(solution)/shard_map/all_to_all | solution.py:70
  80.3 4.0 scatter_custom_fusion.2
  84.3 0.2 convert_reduce_fusion
  84.5 0.3 fusion.26
  84.9 5.1 convolution_convert_fusion
  90.0 0.9 fusion.120
  91.0 2.0 copy.31
  93.0 1.9 copy.29
  95.0 0.7 all-gather.11.cloned.1.call-update
  95.7 0.2 all-gather.13.cloned.1.call-start
  95.9 0.3 all-gather.13.cloned.1.call-update
  96.3 0.7 reduce.72
  97.0 0.1 pad_dynamic-slice_fusion
  97.1 0.7 compare_convert_fusion.31
  97.8 0.7 compare_convert_fusion.30
  98.5 0.1 reshape_squeeze.7
  98.6 0.2 slice_reduce_fusion.32
  98.7 0.2 copy.30
  98.9 21.1 %all-gather.9.cloned.1.call-done = bf16[1024,8,96]{0,2,1:T(8,128)(2,1)} async-done(((bf16[256,8,96]{0,2,1:T(8,128)(2,1)}), bf16[1024,8,96]{0,2,1:T(8,128)(2,1)}) %all-gather.9.cloned.1.call-update) | async-done | bytes 1572880 | tf_op jit(solution)/shard_map/all_gather | solution.py:128
  120.0 2.7 copy.43
  122.7 27.3 %all-gather.7.cloned.1.call-done = bf16[1024,8,96]{0,2,1:T(8,128)(2,1)} async-done(((bf16[256,8,96]{0,2,1:T(8,128)(2,1)}), bf16[1024,8,96]{0,2,1:T(8,128)(2,1)}) %all-gather.7.cloned.1.call-update) | async-done | bytes 1572880 | tf_op jit(solution)/shard_map/all_gather | solution.py:127
  150.1 2.7 copy.44
  152.8 22.4 %while.15 = (s32[]{:T(128)}, f32[8,256]{1,0:T(8,128)S(1)}, f32[8,256]{1,0:T(8,128)S(1)}, f32[8,256,96]{1,2,0:T(8,128)}, s32[256]{0:T(256)S(1)}, /*index=5*/s32[2...) while((s32[]{:T(128)}, f32[8,256]{1,0:T(8,128)S(1)}, ...), condition=%wide.region_11.12_spmd.clone, body=%wide.region_8.11_spmd.clone.sunk | while | flops 417146880 | bytes 33564948 | solution.py:142
  152.8 0.1 broadcast_bitcast_fusion.2
  152.9 0.2 bitcast_and_fusion.2
  153.1 4.1 fusion.139
  157.1 3.3 fusion.140
  160.5 0.1 copy-done.1
  160.6 3.3 fusion.142
  164.0 0.2 bitcast_and_fusion.2
  164.1 4.1 fusion.139
  168.2 3.4 fusion.140
  171.6 0.1 copy-done.1
  171.7 3.5 fusion.142
  175.2 1.3 divide_convert_fusion
  176.5 0.1 copy-done.3
  176.6 0.9 fusion.122
  177.5 1.1 copy-done.4
  178.6 0.3 multiply_reduce_fusion
  178.9 391.2 %all-gather.11.cloned.1.call-done = bf16[256,6,1536]{2,1,0:T(8,128)(2,1)} async-done(((bf16[1,6,1536]{2,1,0:T(8,128)(2,1)}), bf16[256,6,1536]{2,1,0:T(8,128)(2,1)}) %all-gather.11.cloned.1.call-update) | async-done | bytes 4718608 | tf_op jit(solution)/shard_map/all_gather | solution.py:155
  570.1 8.5 reshape.317
  578.5 4.2 fusion.31
  582.8 0.2 fusion.111
  583.0 1.9 collective-permute-start
  585.0 4.4 collective-permute-start.1
  589.4 0.1 slice_reduce_fusion.31
  589.7 392.4 %all-gather.13.cloned.1.call-done = bf16[256,6,768]{2,1,0:T(8,128)(2,1)} async-done(((bf16[1,6,768]{2,1,0:T(8,128)(2,1)}), bf16[256,6,768]{2,1,0:T(8,128)(2,1)}) %all-gather.13.cloned.1.call-update) | async-done | bytes 2359312 | tf_op jit(solution)/shard_map/all_gather | solution.py:178
  982.1 5.1 reshape.319
  987.4 9.2 fusion.23
  (91 shorter events, 0.6 us)
Async XLA Ops:
  6.5 169.9 %copy-start = (bf16[768,1536]{1,0:T(8,128)(2,1)S(1)}, bf16[768,1536]{1,0:T(8,128)(2,1)}, u32[]{:S(2)}) copy-start(bf16[768,1536]{1,0:T(8,128)(2,1)} %param.21) | copy-start | bytes 7077892
  11.8 25.8 %all-to-all-start = ((s32[64,1,8]{2,1,0:T(1,128)}), s32[64,1,8]{2,1,0:T(1,128)S(1)}, u32[]{:S(2)}, u32[]{:S(2)}) async-start(s32[64,1,8]{2,1,0:T(1,128)} %bitcast.6), calls=%async_computation | async-start | bytes 65536 | tf_op jit(solution)/shard_map/all_to_all | solution.py:77
  37.6 42.7 %all-to-all-start.1 = ((bf16[64,8,1536]{2,1,0:T(8,128)(2,1)}), bf16[64,8,1536]{2,1,0:T(8,128)(2,1)}, u32[]{:S(2)}, u32[]{:S(2)}) async-start(bf16[64,8,1536]{2,1,0:T(8,128)(2,1)} %bitcast.124), calls=%async_computation.1 | async-start | bytes 3145728 | tf_op jit(solution)/shard_map/all_to_all | solution.py:70
  43.1 76.9 %all-gather.9.cloned.1.call-start = ((), (), s32[]{:S(2)}) async-start(), calls=%async_computation.3 | async-start | bytes 1966080 | tf_op jit(solution)/shard_map/all_gather | solution.py:128
  80.3 4.5 copy-start.25
  84.3 5.7 copy-start.2
  91.0 5.3 copy-start.6
  91.0 7.5 copy-start.7
  91.0 7.6 copy-start.5
  93.0 57.1 %all-gather.7.cloned.1.call-start = ((), (), s32[]{:S(2)}) async-start(), calls=%async_computation.2 | async-start | bytes 1966080 | tf_op jit(solution)/shard_map/all_gather | solution.py:127
  94.9 475.1 %all-gather.11.cloned.1.call-start = ((), (), s32[]{:S(2)}) async-start(), calls=%async_computation.4 | async-start | bytes 6316032 | tf_op jit(solution)/shard_map/all_gather | solution.py:155
  95.7 886.4 %all-gather.13.cloned.1.call-start = ((), (), s32[]{:S(2)}) async-start(), calls=%async_computation.5 | async-start | bytes 3158016 | tf_op jit(solution)/shard_map/all_gather | solution.py:178
  157.1 3.4 copy-start.1
  168.2 3.5 copy-start.1
  175.2 1.4 copy-start.3
  177.4 1.1 copy-start.4
  178.9 399.6 %copy-start.26 = (f32[1536]{0:T(1024)S(1)}, f32[1536]{0:T(1024)}, u32[]{:S(2)}) copy-start(f32[1536]{0:T(1024)} %param.22) | copy-start | bytes 18436
  583.0 404.1 %collective-permute-start = (bf16[16,768]{1,0:T(8,128)(2,1)S(1)}, bf16[16,768]{1,0:T(8,128)(2,1)S(1)}, u32[]{:S(2)}, u32[]{:S(2)}) collective-permute-start(bf16[16,768]{1,0:T(8,128)(2,1)S(1)} %get-tuple-element.182), channel_id=1, source_target_pairs={{0,1},{1,2},{2,3},{4,5},{5,6},{6,7},{8,9},{9,10},{10,11},{12,13},{... | collective-permute-start | bytes 73736 | tf_op jit(solution)/shard_map/ppermute | solution.py:19
  585.0 402.2 %collective-permute-start.1 = (bf16[16,768]{1,0:T(8,128)(2,1)S(1)}, bf16[16,768]{1,0:T(8,128)(2,1)S(1)}, u32[]{:S(2)}, u32[]{:S(2)}) collective-permute-start(bf16[16,768]{1,0:T(8,128)(2,1)S(1)} %get-tuple-element.183), channel_id=1, source_target_pairs={{1,0},{2,1},{3,2},{5,4},{6,5},{7,6},{9,8},{10,9},{11,10},{13,12},{... | collective-permute-start | bytes 73736 | tf_op jit(solution)/shard_map/ppermute | solution.py:21
  589.5 397.8 %copy-start.8 = (f32[256]{0:T(256)S(1)}, f32[256]{0:T(256)}, u32[]{:S(2)}) copy-start(f32[256]{0:T(256)} %get-tuple-element.199) | copy-start | bytes 3076
  589.5 397.8 %copy-start.9 = (f32[256]{0:T(256)S(1)}, f32[256]{0:T(256)}, u32[]{:S(2)}) copy-start(f32[256]{0:T(256)} %get-tuple-element.200) | copy-start | bytes 3076
  589.5 397.8 %copy-start.10 = (f32[256]{0:T(256)S(1)}, f32[256]{0:T(256)}, u32[]{:S(2)}) copy-start(f32[256]{0:T(256)} %get-tuple-element.201) | copy-start | bytes 3076
  589.5 397.8 %copy-start.11 = (f32[256]{0:T(256)S(1)}, f32[256]{0:T(256)}, u32[]{:S(2)}) copy-start(f32[256]{0:T(256)} %get-tuple-element.202) | copy-start | bytes 3076
  589.5 397.8 %copy-start.12 = (f32[256]{0:T(256)S(1)}, f32[256]{0:T(256)}, u32[]{:S(2)}) copy-start(f32[256]{0:T(256)} %get-tuple-element.203) | copy-start | bytes 3076
  589.5 397.8 %copy-start.13 = (f32[256]{0:T(256)S(1)}, f32[256]{0:T(256)}, u32[]{:S(2)}) copy-start(f32[256]{0:T(256)} %get-tuple-element.204) | copy-start | bytes 3076
  589.5 397.8 %copy-start.14 = (f32[256]{0:T(256)S(1)}, f32[256]{0:T(256)}, u32[]{:S(2)}) copy-start(f32[256]{0:T(256)} %get-tuple-element.205) | copy-start | bytes 3076
  589.5 397.8 %copy-start.15 = (f32[256]{0:T(256)S(1)}, f32[256]{0:T(256)}, u32[]{:S(2)}) copy-start(f32[256]{0:T(256)} %get-tuple-element.206) | copy-start | bytes 3076
  589.5 397.8 %copy-start.16 = (f32[256]{0:T(256)S(1)}, f32[256]{0:T(256)}, u32[]{:S(2)}) copy-start(f32[256]{0:T(256)} %get-tuple-element.207) | copy-start | bytes 3076
  589.6 397.8 %copy-start.17 = (f32[256]{0:T(256)S(1)}, f32[256]{0:T(256)}, u32[]{:S(2)}) copy-start(f32[256]{0:T(256)} %get-tuple-element.208) | copy-start | bytes 3076
  589.6 397.8 %copy-start.18 = (f32[256]{0:T(256)S(1)}, f32[256]{0:T(256)}, u32[]{:S(2)}) copy-start(f32[256]{0:T(256)} %get-tuple-element.209) | copy-start | bytes 3076
  589.6 397.8 %copy-start.19 = (f32[256]{0:T(256)S(1)}, f32[256]{0:T(256)}, u32[]{:S(2)}) copy-start(f32[256]{0:T(256)} %get-tuple-element.210) | copy-start | bytes 3076
  589.6 397.8 %copy-start.20 = (f32[256]{0:T(256)S(1)}, f32[256]{0:T(256)}, u32[]{:S(2)}) copy-start(f32[256]{0:T(256)} %get-tuple-element.211) | copy-start | bytes 3076
  589.6 397.8 %copy-start.21 = (f32[256]{0:T(256)S(1)}, f32[256]{0:T(256)}, u32[]{:S(2)}) copy-start(f32[256]{0:T(256)} %get-tuple-element.212) | copy-start | bytes 3076
  589.6 397.8 %copy-start.22 = (f32[256]{0:T(256)S(1)}, f32[256]{0:T(256)}, u32[]{:S(2)}) copy-start(f32[256]{0:T(256)} %get-tuple-element.213) | copy-start | bytes 3076
  589.6 397.8 %copy-start.23 = (f32[256]{0:T(256)S(1)}, f32[256]{0:T(256)}, u32[]{:S(2)}) copy-start(f32[256]{0:T(256)} %get-tuple-element.214) | copy-start | bytes 3076
  589.6 397.8 %copy-start.24 = (f32[256]{0:T(256)S(1)}, f32[256]{0:T(256)}, u32[]{:S(2)}) copy-start(f32[256]{0:T(256)} %get-tuple-element.215) | copy-start | bytes 3076
  589.6 397.8 %copy-start.27 = (f32[768]{0:T(1024)S(1)}, f32[768]{0:T(1024)}, u32[]{:S(2)}) copy-start(f32[768]{0:T(1024)} %param.27) | copy-start | bytes 9220
  589.7 397.8 %copy-start.28 = (f32[768]{0:T(1024)S(1)}, f32[768]{0:T(1024)}, u32[]{:S(2)}) copy-start(f32[768]{0:T(1024)} %param.26) | copy-start | bytes 9220
Sparse Core Ops, SparseCore 0:
  93.1 26.8 all-gather.8
  121.8 28.2 all-gather.6
  152.0 418.0 all-gather.10
  571.8 410.2 all-gather.12
where the time goes:
time: 1000 us
  waiting for transfers between devices  876 us (88%)
  local copies, waits for them, and re-layouts  36.8 us (4%)
  matrix products  34.4 us (3%)
  starting transfers between devices  27.3 us (3%)
  other arithmetic  15.3 us (2%)
  between operations  13.7 us (1%)
    all_gather x1, waiting for transfers between devices, per_device(): lax.all_gather(w_pointout, ('dp', 'ctx'), axis=1, tiled=True)  392 us
    all_gather x1, waiting for transfers between devices, per_device(): lax.all_gather(w_pointin, ('dp', 'ctx'), axis=0, tiled=True)  391 us
    all_to_all x1, waiting for transfers between devices, per_device(): lax.all_to_all(send_rows.reshape(peer_count, capacity, width), 'dp', spli...  35.7 us
    all_gather x1, waiting for transfers between devices, per_device(): keys_piece = lax.all_gather(key_rows, 'ctx', axis=0, tiled=True)  27.3 us
    all_gather x1, waiting for transfers between devices, per_device(): values_piece = lax.all_gather(value_rows, 'ctx', axis=0, tiled=True)  21.1 us
  transfers between devices with their start and end apart: 8, of which 6 were waited for; matrix products, arithmetic and copies ran while one was open for 6% of the time, Pallas kernels for 0%

commit v1 on v0

v1 whole, which is shorter than its diff:
```python
import math

import numpy as np

import jax
import jax.numpy as jnp
from jax import lax
from jax.experimental import pallas as pl
from jax.experimental.pallas import tpu as pltpu
from jax.sharding import PartitionSpec as P

HEADS = 8
NX = 4
NY = 2
MESH = pl.DeviceIdType.MESH
BF = jnp.bfloat16
F32 = jnp.float32
MASKED = -2e38


def dot(a, b):
    return jnp.dot(a, b, preferred_element_type=F32)


def dot_nt(a, b):
    return lax.dot_general(a, b, (((1,), (1,)), ((), ())), preferred_element_type=F32)


def layer_norm(as_float, gain):
    row_mean = jnp.mean(as_float, axis=-1, keepdims=True)
    centred = as_float - row_mean
    row_var = jnp.mean(centred * centred, axis=-1, keepdims=True)
    return centred * lax.rsqrt(row_var + 1e-06) * gain


def layer_kernel(
    n_dp,
    shard_rows,
    dest_ref,
    frames_ref,
    seg_ref,
    tile_ref,
    again_ref,
    wqkv_hbm,
    wout_hbm,
    cgain_ref,
    shard_ref,
    pick_ref,
    wdepth_ref,
    bns_ref,
    bnb_ref,
    out_ref,
    wqkv_ref,
    wout_ref,
    send_ref,
    got_ref,
    zbuf_ref,
    cbuf_ref,
    wfull_ref,
    kv_ref,
    q_ref,
    att_ref,
    placed_ref,
    after_ref,
    bias_ref,
    segc_ref,
    segn_ref,
    mask_ref,
    gat_ref,
    htop_ref,
    hbot_ref,
    gf_ref,
    act_ref,
    load_sem,
    a_send,
    a_recv,
    bz_send,
    bz_recv,
    bc_send,
    bc_recv,
    by_send,
    by_recv,
    bx_send,
    bx_recv,
    sib_send,
    sib_recv,
    kv_send,
    kv_recv,
    halo_send,
    halo_recv,
):
    rows, width = frames_ref.shape
    seq = seg_ref.shape[1]
    nz = n_dp // (NX * NY)
    cap = send_ref.shape[1]
    head_cols = wout_ref.shape[0]
    head = head_cols // HEADS
    group = head_cols // 2
    half_cols = cbuf_ref.shape[3]
    block = NY * 0 + wfull_ref.shape[1] // (NX * NY)
    channels = wdepth_ref.shape[1]
    taps = wdepth_ref.shape[0]
    half = taps // 2
    tile = 128

    dp = lax.axis_index("dp")
    ctx = lax.axis_index("ctx")
    x = dp // (NY * nz)
    yh = (dp // nz) % NY
    z = dp % nz
    core = ctx % 2

    def dp_of(px, py, pz):
        return (px * NY + py) * nz + pz

    def peer(k):
        kx, ky, kz = k // (NY * nz), (k // nz) % NY, k % nz
        return dp_of((x + kx) % NX, (yh + ky) % NY, (z + kz) % nz)

    def put(src, dst, ssem, rsem, d, c):
        copy = pltpu.make_async_remote_copy(
            src_ref=src, dst_ref=dst, send_sem=ssem, recv_sem=rsem, device_id=(d, c), device_id_type=MESH
        )
        copy.start()

    def settle(ref, sem):
        pltpu.make_async_copy(ref, ref, sem).wait()

    barrier = pltpu.get_barrier_semaphore()

    def greet(k, carry):
        pl.semaphore_signal(barrier, inc=1, device_id=(peer(k), ctx), device_id_type=MESH)
        return carry

    lax.fori_loop(1, n_dp, greet, 0)
    for d in range(1, 4):
        pl.semaphore_signal(barrier, inc=1, device_id=(dp, ctx ^ d), device_id_type=MESH)

    load_qkv = pltpu.make_async_copy(wqkv_hbm, wqkv_ref, load_sem.at[0])
    load_qkv.start()
    load_out = pltpu.make_async_copy(wout_hbm, wout_ref, load_sem.at[1])
    load_out.start()

    dest = dest_ref[...]
    owner = dest // rows
    slot = dest % rows
    oz = owner % nz
    oy = (owner // nz) % NY
    ox = owner // (nz * NY)
    rel = (((ox - x + NX) % NX) * NY + (oy - yh + NY) % NY) * nz + (oz - z + nz) % nz
    rel_wide = jnp.broadcast_to(rel.astype(F32), (rows, rows))
    rel_tall = jnp.transpose(rel_wide)
    earlier = lax.broadcasted_iota(jnp.int32, (rows, rows), 0) < lax.broadcasted_iota(jnp.int32, (rows, rows), 1)
    rank = jnp.sum(jnp.where((rel_tall == rel_wide) & earlier, 1.0, 0.0), axis=0, keepdims=True)
    pos = rel * cap + rank.astype(jnp.int32)
    slot_tall = jnp.transpose(jnp.broadcast_to(slot.astype(F32) + 1.0, (tile, rows))).astype(BF)
    frames = frames_ref[...]
    zbuf_ref[pl.ds(z, 1)] = shard_ref[...]

    parts = 4
    per = n_dp // parts
    for c in range(parts):
        chunk = lax.broadcasted_iota(jnp.int32, (per * cap, rows), 0) + c * per * cap
        onehot = jnp.where(chunk == pos, 1.0, 0.0).astype(BF)
        send_ref[c * per : (c + 1) * per, :, :width] = dot(onehot, frames).reshape(per, cap, width).astype(BF)
        send_ref[c * per : (c + 1) * per, :, width:] = dot(onehot, slot_tall).reshape(per, cap, tile).astype(BF)
        if c == 0:
            pl.semaphore_wait(barrier, n_dp - 1 + 3)
            for k in range(1, nz):
                put(
                    zbuf_ref.at[z], zbuf_ref.at[z], bz_send.at[k], bz_recv.at[k], dp_of(x, yh, (z + k) % nz), ctx
                )
            got_ref[0:1] = send_ref[0:1]

        def ship(k, carry):
            put(send_ref.at[k], got_ref.at[k], a_send, a_recv, peer(k), ctx)
            return carry

        lax.fori_loop(max(1, c * per), (c + 1) * per, ship, 0)

    segf = seg_ref[...].astype(F32)
    segc_ref[0:half] = jnp.full((half, tile), -1.0, F32)
    segc_ref[half + seq :] = jnp.full((half, tile), -1.0, F32)
    segc_ref[half : half + seq] = jnp.transpose(jnp.broadcast_to(segf, (tile, seq)))
    first = pl.multiple_of(ctx * rows, rows)
    segn_ref[...] = segc_ref[pl.ds(first, rows + 2 * half)]
    own_seg = segn_ref[half : half + rows]
    for tk in range(seq // tile):
        same = own_seg == segf[:, tk * tile : (tk + 1) * tile]
        for tq in range(rows // tile):
            off = (1 - tile_ref[tq, tk]).astype(F32) * MASKED
            bias_ref[tq * tile : (tq + 1) * tile, tk * tile : (tk + 1) * tile] = jnp.where(
                same[tq * tile : (tq + 1) * tile], off, MASKED
            )
    for k in range(taps):
        mask_ref[k] = jnp.where(segn_ref[k : k + rows] == own_seg, 1.0, 0.0)

    for k in range(1, nz):
        settle(zbuf_ref.at[0], bz_recv.at[k])
    for d in range(1, 4):
        cols = pl.ds(pl.multiple_of(((ctx ^ d) % 2) * half_cols, 128), half_cols)
        put(zbuf_ref.at[:, :, cols], cbuf_ref.at[ctx], bc_send.at[d], bc_recv.at[d], dp, ctx ^ d)
    mine = pl.ds(pl.multiple_of(core * half_cols, 128), half_cols)
    cbuf_ref[pl.ds(ctx, 1)] = zbuf_ref[:, :, mine][None]
    for d in range(1, 4):
        settle(cbuf_ref.at[0], bc_recv.at[d])
    padded = cbuf_ref[...].astype(F32).reshape(pick_ref.shape[1], half_cols).astype(BF)

    def piece(px, py):
        start = pl.multiple_of((((px + NX) % NX) * NY + py) * block, 16)
        return wfull_ref.at[core, pl.ds(start, block)]

    own_start = pl.multiple_of((x * NY + yh) * block, 16)
    wfull_ref[core, pl.ds(own_start, block)] = dot(pick_ref[...], padded).astype(BF)
    right = dp_of((x + 1) % NX, yh, z)
    left = dp_of((x + NX - 1) % NX, yh, z)
    other = 1 - yh

    def to_sibling(i, ref):
        put(ref, ref, sib_send.at[i], sib_recv.at[i], dp, ctx ^ 1)

    put(piece(x, yh), piece(x, yh), by_send, by_recv, dp_of(x, other, z), ctx)
    put(piece(x, yh), piece(x, yh), bx_send.at[0], bx_recv.at[0], right, ctx)
    put(piece(x, yh), piece(x, yh), bx_send.at[1], bx_recv.at[1], left, ctx)
    to_sibling(0, piece(x, yh))

    settle(got_ref.at[pl.ds(1, n_dp - 1)], a_recv)
    got = got_ref[...].astype(F32).reshape(n_dp * cap, width + tile)
    slots = jnp.transpose(got[:, width:])[0:1]
    lane = lax.broadcasted_iota(jnp.int32, (rows, n_dp * cap), 0).astype(F32) + 1.0
    place = jnp.where(lane == slots, 1.0, 0.0).astype(BF)
    placed = dot(place, got[:, :width].astype(BF))
    placed_ref[...] = placed
    normed = layer_norm(placed, again_ref[...]).astype(BF)

    load_qkv.wait()
    base = pl.multiple_of(ctx * rows, rows)
    keys = dot(normed, wqkv_ref[:, head_cols : 2 * head_cols]).astype(BF)
    values = dot(normed, wqkv_ref[:, 2 * head_cols :]).astype(BF)
    for g in range(2):
        kv_ref[pl.ds(base, rows), 2 * g * group : (2 * g + 1) * group] = keys[:, g * group : (g + 1) * group]
        kv_ref[pl.ds(base, rows), (2 * g + 1) * group : (2 * g + 2) * group] = values[:, g * group : (g + 1) * group]

    def kv_part(c, g):
        return kv_ref.at[pl.ds(pl.multiple_of(c * rows, rows), rows), pl.ds(2 * g * group, 2 * group)]

    for g in range(2):
        part = kv_part(ctx, g)
        put(part, part, kv_send.at[g, 0], kv_recv.at[g, 0], dp, ctx ^ 2)
        put(part, part, kv_send.at[g, 1], kv_recv.at[g, 1], dp, ctx ^ 1)
    scale = math.log2(math.e) / math.sqrt(head)
    q_ref[...] = (dot(normed, wqkv_ref[:, :head_cols]) * scale).astype(BF)

    settle(piece(x, other), by_recv)
    put(piece(x, other), piece(x, other), bx_send.at[2], bx_recv.at[2], right, ctx)
    put(piece(x, other), piece(x, other), bx_send.at[3], bx_recv.at[3], left, ctx)
    to_sibling(1, piece(x, other))

    def attend(g):
        settle(kv_part(ctx ^ 2, g), kv_recv.at[g, 0])
        part = kv_part(ctx ^ 2, g)
        put(part, part, kv_send.at[g, 2], kv_recv.at[g, 2], dp, ctx ^ 1)
        settle(part, kv_recv.at[g, 1])
        settle(part, kv_recv.at[g, 2])
        tiles = [None] * (group // tile)
        for h in range(HEADS // 2):
            lo, hi = h * head, (h + 1) * head
            t0, t1 = lo // tile, (hi + tile - 1) // tile
            c0, c1 = t0 * tile, t1 * tile
            lanes = lax.broadcasted_iota(jnp.int32, (rows, c1 - c0), 1) + c0
            inside = (lanes >= lo) & (lanes < hi)
            query = q_ref[:, g * group + c0 : g * group + c1].astype(F32)
            query = jnp.where(inside, query, 0.0).astype(BF)
            scores = dot_nt(query, kv_ref[:, 2 * g * group + c0 : 2 * g * group + c1]) + bias_ref[...]
            top = jnp.max(scores, axis=1, keepdims=True)
            weights = jnp.exp2(scores - top)
            total = jnp.sum(weights, axis=1, keepdims=True)
            mixed = dot(weights.astype(BF), kv_ref[:, (2 * g + 1) * group + c0 : (2 * g + 1) * group + c1])
            mixed = jnp.where(inside, mixed / total, 0.0)
            for t in range(t0, t1):
                term = mixed[:, (t - t0) * tile : (t - t0 + 1) * tile]
                tiles[t] = term if tiles[t] is None else tiles[t] + term
        for t, whole in enumerate(tiles):
            att_ref[:, g * group + t * tile : g * group + (t + 1) * tile] = whole.astype(BF)

    attend(0)
    settle(piece(x - 1, yh), bx_recv.at[0])
    settle(piece(x + 1, yh), bx_recv.at[1])
    put(piece(x - 1, yh), piece(x - 1, yh), bx_send.at[4], bx_recv.at[4], right, ctx)
    to_sibling(2, piece(x - 1, yh))
    to_sibling(3, piece(x + 1, yh))
    attend(1)
    settle(piece(x - 1, other), bx_recv.at[2])
    settle(piece(x + 1, other), bx_recv.at[3])
    put(piece(x + 1, other), piece(x + 1, other), bx_send.at[5], bx_recv.at[5], left, ctx)
    to_sibling(4, piece(x - 1, other))
    to_sibling(5, piece(x + 1, other))

    load_out.wait()
    after = (placed_ref[...] + dot(att_ref[...], wout_ref[...])).astype(BF)
    after_ref[...] = after
    conv_normed = layer_norm(after.astype(F32), cgain_ref[...]).astype(BF)

    settle(piece(x + 2, yh), bx_recv.at[4])
    to_sibling(6, piece(x + 2, yh))
    settle(piece(x + 2, other), bx_recv.at[5])
    to_sibling(7, piece(x + 2, other))
    for i in range(NX * NY):
        settle(piece(x, yh), sib_recv.at[i])

    gate = jax.nn.sigmoid(dot(conv_normed, wfull_ref[1, :, :channels]))
    gated = (dot(conv_normed, wfull_ref[0, :, :channels]) * gate).astype(BF)
    gat_ref[...] = gated
    gf_ref[half : half + rows] = gated.astype(F32)

    head_rows = gat_ref.at[0:half]
    tail_rows = gat_ref.at[rows - half : rows]

    @pl.when(ctx > 0)
    def _():
        put(head_rows, hbot_ref, halo_send.at[0], halo_recv.at[0], dp, ctx - 1)

    @pl.when(ctx < 3)
    def _():
        put(tail_rows, htop_ref, halo_send.at[1], halo_recv.at[1], dp, ctx + 1)

    @pl.when(ctx == 0)
    def _():
        htop_ref[...] = jnp.zeros_like(htop_ref)

    @pl.when(ctx == 3)
    def _():
        hbot_ref[...] = jnp.zeros_like(hbot_ref)

    span = 64

    def convolve(r0):
        def body(t, carry):
            lanes = pl.ds(pl.multiple_of(t * tile, tile), tile)
            near = gf_ref[r0 : r0 + span + 2 * half, lanes]
            total = jnp.zeros((span, tile), F32)
            for b in range(8):
                shifted = near if b == 0 else pltpu.roll(near, span + 2 * half - b, 0)
                for a in range(taps // 8):
                    k = 8 * a + b
                    term = shifted[8 * a : 8 * a + span] * mask_ref[k, r0 : r0 + span]
                    total = total + term * wdepth_ref[k : k + 1, lanes]
            moved = total * bns_ref[:, lanes] + bnb_ref[:, lanes]
            act_ref[r0 : r0 + span, lanes] = (moved * jax.nn.sigmoid(moved)).astype(BF)
            return carry

        lax.fori_loop(0, channels // tile, body, 0)

    for r0 in range(span, rows - span, span):
        convolve(r0)

    @pl.when(ctx > 0)
    def _():
        settle(htop_ref, halo_recv.at[1])

    @pl.when(ctx < 3)
    def _():
        settle(hbot_ref, halo_recv.at[0])

    gf_ref[0:half] = htop_ref[...].astype(F32)
    gf_ref[half + rows :] = hbot_ref[...].astype(F32)
    convolve(0)
    convolve(rows - span)

    quarter = channels // 2
    closing = dot_nt(act_ref[:, :quarter], wfull_ref[0, :, channels:])
    closing = closing + dot_nt(act_ref[:, quarter:], wfull_ref[1, :, channels:])
    out_ref[...] = (after_ref[...].astype(F32) + closing).astype(BF)

    settle(send_ref.at[pl.ds(1, n_dp - 1)], a_send)
    for k in range(1, nz):
        settle(zbuf_ref.at[0], bz_send.at[k])
    for d in range(1, 4):
        settle(cbuf_ref.at[0], bc_send.at[d])
    settle(piece(x, yh), by_send)
    for i in range(6):
        settle(piece(x, yh), bx_send.at[i])
    for i in range(NX * NY):
        settle(piece(x, yh), sib_send.at[i])
    for g in range(2):
        for i in range(3):
            settle(kv_part(ctx, g), kv_send.at[g, i])

    @pl.when(ctx > 0)
    def _():
        settle(head_rows, halo_send.at[0])

    @pl.when(ctx < 3)
    def _():
        settle(tail_rows, halo_send.at[1])


def solution(mesh):
    n_dp = mesh.shape["dp"]
    n_ctx = mesh.shape["ctx"]
    nz = n_dp // (NX * NY)

    def per_device(
        frames,
        destinations,
        segments,
        tile_mask,
        attn_gain,
        w_qkv,
        w_out,
        conv_gain,
        w_pointin,
        w_pointout,
        w_depth,
        bn_scale,
        bn_shift,
    ):
        rows, width = frames.shape[1:]
        seq = segments.shape[1]
        channels = w_depth.shape[1]
        taps = w_depth.shape[0]
        head_cols = w_out.shape[0]
        cap = 2 * rows // n_dp
        shard_rows = w_pointin.shape[0]
        pad_rows = -(-shard_rows // 8) * 8
        half_cols = channels + channels // 2
        flipped = w_pointout.T
        shard = jnp.concatenate(
            [
                w_pointin[:, :channels],
                flipped[:, : channels // 2],
                w_pointin[:, channels:],
                flipped[:, channels // 2 :],
            ],
            axis=1,
        )
        shard = jnp.pad(shard, ((0, pad_rows - shard_rows), (0, 0)))[None]
        pick = np.zeros((nz * n_ctx * shard_rows, n_ctx * nz * pad_rows), np.float32)
        for a in range(nz):
            for b in range(n_ctx):
                for j in range(shard_rows):
                    pick[(a * n_ctx + b) * shard_rows + j, (b * nz + a) * pad_rows + j] = 1.0
        pick = jnp.asarray(pick, BF)
        vmem = pl.BlockSpec(memory_space=pltpu.VMEM)
        smem = pl.BlockSpec(memory_space=pltpu.SMEM)
        hbm = pl.BlockSpec(memory_space=pl.ANY)

        def body(*refs):
            layer_kernel(n_dp, shard_rows, *refs)

        dma = pltpu.SemaphoreType.DMA
        out = pl.pallas_call(
            body,
            name="conformer_layer",
            out_shape=jax.ShapeDtypeStruct((rows, width), BF),
            in_specs=[vmem, vmem, vmem, smem, vmem, hbm, hbm] + [vmem] * 6,
            out_specs=vmem,
            scratch_shapes=[
                pltpu.VMEM(w_qkv.shape, BF),
                pltpu.VMEM(w_out.shape, BF),
                pltpu.VMEM((n_dp, cap, width + 128), BF),
                pltpu.VMEM((n_dp, cap, width + 128), BF),
                pltpu.VMEM((nz, pad_rows, 2 * half_cols), BF),
                pltpu.VMEM((n_ctx, nz, pad_rows, half_cols), BF),
                pltpu.VMEM((2, width, half_cols), BF),
                pltpu.VMEM((seq, 2 * head_cols), BF),
                pltpu.VMEM((rows, head_cols), BF),
                pltpu.VMEM((rows, head_cols), BF),
                pltpu.VMEM((rows, width), F32),
                pltpu.VMEM((rows, width), BF),
                pltpu.VMEM((rows, seq), F32),
                pltpu.VMEM((seq + taps, 128), F32),
                pltpu.VMEM((rows + taps, 128), F32),
                pltpu.VMEM((taps, rows, 128), F32),
                pltpu.VMEM((rows, channels), BF),
                pltpu.VMEM((taps // 2, channels), BF),
                pltpu.VMEM((taps // 2, channels), BF),
                pltpu.VMEM((rows + taps, channels), F32),
                pltpu.VMEM((rows, channels), BF),
                dma((2,)),
                dma,
                dma,
                dma((8,)),
                dma((8,)),
                dma((4,)),
                dma((4,)),
                dma,
                dma,
                dma((6,)),
                dma((6,)),
                dma((NX * NY,)),
                dma((NX * NY,)),
                dma((2, 3)),
                dma((2, 3)),
                dma((2,)),
                dma((2,)),
            ],
            compiler_params=pltpu.CompilerParams(
                collective_id=0, has_side_effects=True, vmem_limit_bytes=60 * 2**20
            ),
            cost_estimate=pl.CostEstimate(flops=6 * 10**9, bytes_accessed=20 * 10**6, transcendentals=3 * 10**6),
        )(
            destinations,
            frames[0],
            segments,
            tile_mask[0],
            attn_gain[None],
            w_qkv,
            w_out,
            conv_gain[None],
            shard,
            pick,
            w_depth,
            bn_scale[None],
            bn_shift[None],
        )
        return out[None]

    return jax.shard_map(
        per_device,
        mesh=mesh,
        in_specs=(
            P("dp", "ctx", None),
            P("dp", "ctx"),
            P("dp", None),
            P("dp", "ctx", None),
            P(),
            P(),
            P(),
            P(),
            P(("dp", "ctx"), None),
            P(None, ("dp", "ctx")),
            P(),
            P(),
            P(),
        ),
        out_specs=P("dp", "ctx", None),
        check_vma=False,
    )
```

time: 1000 us -> 113 us (0.11)
  waiting for transfers between devices: 876 us -> 0 us
  Pallas kernels: 0 us -> 104 us
  matrix products: 34.4 us -> 0 us
  local copies, waits for them, and re-layouts: 36.8 us -> 8.63 us
  starting transfers between devices: 27.3 us -> 0 us
  other arithmetic: 15.3 us -> 0.63 us
  between operations: 13.7 us -> 0.01 us
    all_gather x4 -> x0, waiting for transfers between devices: 832 us -> none  [the longest x1 392 us: per_device(): lax.all_gather(w_pointout, ('dp', 'ctx'), axis=1, tiled=True)]
    pallas_call x0 -> x1, Pallas kernels: none -> 104 us  [per_device(): pl.pallas_call(body, name='conformer_layer', out_shape=jax.ShapeDtypeStru...]
    all_to_all x2 -> x0, waiting for transfers between devices: 42.6 us -> none  [the longest x1 35.7 us: per_device(): lax.all_to_all(send_rows.reshape(peer_count, capacity, width), 'dp', spli...]
    dot_general x8 -> x0, matrix products: 34.4 us -> none  [the longest x1 9.22 us: per_device(): jnp.dot(activated, lax.all_gather(w_pointout, ('dp', 'ctx'), axis=1, tile...]
    all_to_all x2 -> x0, starting transfers between devices: 20.6 us -> none  [the longest x1 15.1 us: per_device(): lax.all_to_all(send_slots.reshape(peer_count, capacity), 'dp', split_axis...]
    unnamed x59 -> x1, local copies, waits for them, and re-layouts: 15.5 us -> 2.06 us
  transfers between devices with their start and end apart: 8 -> 0, of which waited for: 6 -> 0; matrix products, arithmetic and copies ran while one was open for 6% -> 0% of each run, Pallas kernels for 0% -> 0%
where the time goes in v1:
time: 113 us
  Pallas kernels  104 us (92%)
  local copies, waits for them, and re-layouts  8.63 us (8%)
    pallas_call x1, Pallas kernels, per_device(): pl.pallas_call(body, name='conformer_layer', out_shape=jax.ShapeDtypeStru...  104 us

profile of v1, /device:TPU:1, one launch (start us, length us, event | category | flops | bytes accessed | tf_op | source)
XLA Modules:
  0.0 112.9 jit_solution(18118074381919394977)
XLA Ops:
  0.0 1.3 %broadcast_in_dim.21.refs_11_ = f32[1,768]{1,0:T(1,128)} reshape(f32[768]{0:T(1024)} %param.25) | data formatting | bytes 6144 | tf_op jit(solution)/shard_map/broadcast_in_dim | solution.py:514
  1.3 1.3 %broadcast_in_dim.22.refs_12_ = f32[1,768]{1,0:T(1,128)} reshape(f32[768]{0:T(1024)} %param.26) | data formatting | bytes 6144 | tf_op jit(solution)/shard_map/broadcast_in_dim | solution.py:515
  2.6 1.3 %broadcast_in_dim.18.refs_4_ = f32[1,1536]{1,0:T(1,128)} reshape(f32[1536]{0:T(1024)} %param.18) | data formatting | bytes 12288 | tf_op jit(solution)/shard_map/broadcast_in_dim | solution.py:507
  3.9 1.3 %broadcast_in_dim.19.refs_7_ = f32[1,1536]{1,0:T(1,128)} reshape(f32[1536]{0:T(1024)} %param.21) | data formatting | bytes 12288 | tf_op jit(solution)/shard_map/broadcast_in_dim | solution.py:510
  5.1 0.7 fusion.9
  5.8 0.7 fusion.8
  6.6 0.6 fusion.7.refs_8_
  7.2 103.7 %conformer_layer.1 = bf16[256,1536]{1,0:T(8,128)(2,1)} custom-call(s32[1,256]{1,0:T(1,128)} %refs_0_.1, bf16[256,1536]{1,0:T(8,128)(2,1)} %bitcast.8, s32[1,1024]{1,0:T(1,128)} %refs_2_.1, s32[2,8]{1,0:T(2,128)} %bitcast.9, f32[1,1536]{1,0:T(1,128)} %broadcast_in_dim.18.refs_4_, bf16[1536,2304]{1,0:T(8,128)(2,1)} %refs_5_.1, bf16[768,1536]{1,0:T(8,128)(2,1)} %refs_6_.1, ...), custom_call_target="tpu_custom_call" | custom-call | flops 6000000000 | bytes 20000000 | tf_op jit(solution)/shard_map/conformer_layer/pallas_call | solution.py:452
  110.9 2.1 %copy.16 = bf16[1,256,1536]{2,1,0:T(8,128)(2,1)} copy(bf16[1,256,1536]{2,1,0:T(8,128)(2,1)} %bitcast.6) | data formatting | bytes 1572864

commit v2 on v1

--- a/solution.py
+++ b/solution.py
@@ -44,7 +44,8 @@
     wqkv_hbm,
     wout_hbm,
     cgain_ref,
-    shard_ref,
+    pin_ref,
+    pout_ref,
     pick_ref,
     wdepth_ref,
     bns_ref,
@@ -54,6 +55,9 @@
     wout_ref,
     send_ref,
     got_ref,
+    meta_ref,
+    gmeta_ref,
+    prob_ref,
     zbuf_ref,
     cbuf_ref,
     wfull_ref,
@@ -74,6 +78,8 @@
     load_sem,
     a_send,
     a_recv,
+    m_send,
+    m_recv,
     bz_send,
     bz_recv,
     bc_send,
@@ -97,7 +103,7 @@
     head = head_cols // HEADS
     group = head_cols // 2
     half_cols = cbuf_ref.shape[3]
-    block = NY * 0 + wfull_ref.shape[1] // (NX * NY)
+    block = wfull_ref.shape[1] // (NX * NY)
     channels = wdepth_ref.shape[1]
     taps = wdepth_ref.shape[0]
     half = taps // 2
@@ -113,9 +119,10 @@
     def dp_of(px, py, pz):
         return (px * NY + py) * nz + pz
 
-    def peer(k):
-        kx, ky, kz = k // (NY * nz), (k // nz) % NY, k % nz
-        return dp_of((x + kx) % NX, (yh + ky) % NY, (z + kz) % nz)
+    def peer(i):
+        zi, rest = i // (NX * NY), NX * NY - 1 - i % (NX * NY)
+        kz = nz // 2 + ((zi + 1) // 2) * (1 - 2 * (zi % 2))
+        return dp_of((x + rest // NY) % NX, (yh + rest % NY) % NY, (z + kz + nz) % nz)
 
     def put(src, dst, ssem, rsem, d, c):
         copy = pltpu.make_async_remote_copy(
@@ -132,7 +139,7 @@
         pl.semaphore_signal(barrier, inc=1, device_id=(peer(k), ctx), device_id_type=MESH)
         return carry
 
-    lax.fori_loop(1, n_dp, greet, 0)
+    lax.fori_loop(0, n_dp - 1, greet, 0)
     for d in range(1, 4):
         pl.semaphore_signal(barrier, inc=1, device_id=(dp, ctx ^ d), device_id_type=MESH)
 
@@ -147,36 +154,82 @@
     oz = owner % nz
     oy = (owner // nz) % NY
     ox = owner // (nz * NY)
-    rel = (((ox - x + NX) % NX) * NY + (oy - yh + NY) % NY) * nz + (oz - z + nz) % nz
+    dz = (oz - z + nz) % nz - nz // 2
+    zi = jnp.where(dz >= 0, 2 * dz, -2 * dz - 1)
+    rel = (zi + 1) * (NX * NY) - 1 - (((ox - x + NX) % NX) * NY + (oy - yh + NY) % NY)
     rel_wide = jnp.broadcast_to(rel.astype(F32), (rows, rows))
     rel_tall = jnp.transpose(rel_wide)
     earlier = lax.broadcasted_iota(jnp.int32, (rows, rows), 0) < lax.broadcasted_iota(jnp.int32, (rows, rows), 1)
     rank = jnp.sum(jnp.where((rel_tall == rel_wide) & earlier, 1.0, 0.0), axis=0, keepdims=True)
     pos = rel * cap + rank.astype(jnp.int32)
-    slot_tall = jnp.transpose(jnp.broadcast_to(slot.astype(F32) + 1.0, (tile, rows))).astype(BF)
     frames = frames_ref[...]
-    zbuf_ref[pl.ds(z, 1)] = shard_ref[...]
-
-    parts = 4
-    per = n_dp // parts
-    for c in range(parts):
+    per = n_dp // 4
+
+    def pack(c):
         chunk = lax.broadcasted_iota(jnp.int32, (per * cap, rows), 0) + c * per * cap
         onehot = jnp.where(chunk == pos, 1.0, 0.0).astype(BF)
-        send_ref[c * per : (c + 1) * per, :, :width] = dot(onehot, frames).reshape(per, cap, width).astype(BF)
-        send_ref[c * per : (c + 1) * per, :, width:] = dot(onehot, slot_tall).reshape(per, cap, tile).astype(BF)
-        if c == 0:
-            pl.semaphore_wait(barrier, n_dp - 1 + 3)
-            for k in range(1, nz):
-                put(
-                    zbuf_ref.at[z], zbuf_ref.at[z], bz_send.at[k], bz_recv.at[k], dp_of(x, yh, (z + k) % nz), ctx
-                )
-            got_ref[0:1] = send_ref[0:1]
-
-        def ship(k, carry):
-            put(send_ref.at[k], got_ref.at[k], a_send, a_recv, peer(k), ctx)
-            return carry
-
-        lax.fori_loop(max(1, c * per), (c + 1) * per, ship, 0)
+        send_ref[c * per : (c + 1) * per] = dot(onehot, frames).reshape(per, cap, width).astype(BF)
+
+    def ship(i, carry):
+        put(send_ref.at[i], got_ref.at[i], a_send, a_recv, peer(i), ctx)
+        put(meta_ref.at[i], gmeta_ref.at[i], m_send, m_recv, peer(i), ctx)
+        return carry
+
+    def piece(px, py):
+        start = pl.multiple_of((((px + NX) % NX) * NY + py) * block, 16)
+        return wfull_ref.at[core, pl.ds(start, block)]
+
+    right = dp_of((x + 1) % NX, yh, z)
+    left = dp_of((x + NX - 1) % NX, yh, z)
+    other = 1 - yh
+
+    def to_sibling(i, ref):
+        put(ref, ref, sib_send.at[i], sib_recv.at[i], dp, ctx ^ 1)
+
+    zbuf_ref[pl.ds(z, 1)] = jnp.zeros((1,) + zbuf_ref.shape[1:], BF)
+    for c in range(2):
+        left_col = c * half_cols
+        zbuf_ref[pl.ds(z, 1), :shard_rows, left_col : left_col + channels] = pin_ref[
+            :, c * channels : (c + 1) * channels
+        ][None]
+        zbuf_ref[pl.ds(z, 1), :shard_rows, left_col + channels : left_col + half_cols] = pout_ref[
+            :, c * (channels // 2) : (c + 1) * (channels // 2)
+        ][None]
+    pack(0)
+    rank_tall = jnp.transpose(jnp.broadcast_to(rank, (tile, rows)))
+    slot_tall = jnp.transpose(jnp.broadcast_to(slot.astype(F32) + 1.0, (tile, rows)))
+    lane = lax.broadcasted_iota(jnp.int32, (rows, tile), 1).astype(F32)
+    at_rank = jnp.where(rank_tall == lane, slot_tall, 0.0).astype(BF)
+    to_peer = jnp.where(lax.broadcasted_iota(jnp.int32, (n_dp, rows), 0) == rel, 1.0, 0.0).astype(BF)
+    meta_ref[...] = dot(to_peer, at_rank).reshape(n_dp, 1, tile)
+    pl.semaphore_wait(barrier, n_dp - 1 + 3)
+    for k in range(1, nz):
+        put(zbuf_ref.at[z], zbuf_ref.at[z], bz_send.at[k], bz_recv.at[k], dp_of(x, yh, (z + k) % nz), ctx)
+    lax.fori_loop(0, per, ship, 0)
+    pack(1)
+
+    for k in range(1, nz):
+        settle(zbuf_ref.at[0], bz_recv.at[k])
+    for d in range(1, 4):
+        cols = pl.ds(pl.multiple_of(((ctx ^ d) % 2) * half_cols, 128), half_cols)
+        put(zbuf_ref.at[:, :, cols], cbuf_ref.at[ctx], bc_send.at[d], bc_recv.at[d], dp, ctx ^ d)
+    lax.fori_loop(per, 2 * per, ship, 0)
+    mine = pl.ds(pl.multiple_of(core * half_cols, 128), half_cols)
+    cbuf_ref[pl.ds(ctx, 1)] = zbuf_ref[:, :, mine][None]
+    pack(2)
+    pack(3)
+    for d in range(1, 4):
+        settle(cbuf_ref.at[0], bc_recv.at[d])
+    padded = cbuf_ref[...].astype(F32).reshape(pick_ref.shape[1], half_cols).astype(BF)
+    own_start = pl.multiple_of((x * NY + yh) * block, 16)
+    wfull_ref[core, pl.ds(own_start, block)] = dot(pick_ref[...], padded).astype(BF)
+    put(piece(x, yh), piece(x, yh), by_send, by_recv, dp_of(x, other, z), ctx)
+    put(piece(x, yh), piece(x, yh), bx_send.at[0], bx_recv.at[0], right, ctx)
+    put(piece(x, yh), piece(x, yh), bx_send.at[1], bx_recv.at[1], left, ctx)
+    to_sibling(0, piece(x, yh))
+    lax.fori_loop(2 * per, n_dp - 1, ship, 0)
+    got_ref[n_dp - 1] = send_ref[n_dp - 1]
+    gmeta_ref[n_dp - 1] = meta_ref[n_dp - 1]
 
     segf = seg_ref[...].astype(F32)
     segc_ref[0:half] = jnp.full((half, tile), -1.0, F32)
@@ -195,43 +248,29 @@
     for k in range(taps):
         mask_ref[k] = jnp.where(segn_ref[k : k + rows] == own_seg, 1.0, 0.0)
 
-    for k in range(1, nz):
-        settle(zbuf_ref.at[0], bz_recv.at[k])
-    for d in range(1, 4):
-        cols = pl.ds(pl.multiple_of(((ctx ^ d) % 2) * half_cols, 128), half_cols)
-        put(zbuf_ref.at[:, :, cols], cbuf_ref.at[ctx], bc_send.at[d], bc_recv.at[d], dp, ctx ^ d)
-    mine = pl.ds(pl.multiple_of(core * half_cols, 128), half_cols)
-    cbuf_ref[pl.ds(ctx, 1)] = zbuf_ref[:, :, mine][None]
-    for d in range(1, 4):
-        settle(cbuf_ref.at[0], bc_recv.at[d])
-    padded = cbuf_ref[...].astype(F32).reshape(pick_ref.shape[1], half_cols).astype(BF)
-
-    def piece(px, py):
-        start = pl.multiple_of((((px + NX) % NX) * NY + py) * block, 16)
-        return wfull_ref.at[core, pl.ds(start, block)]
-
-    own_start = pl.multiple_of((x * NY + yh) * block, 16)
-    wfull_ref[core, pl.ds(own_start, block)] = dot(pick_ref[...], padded).astype(BF)
-    right = dp_of((x + 1) % NX, yh, z)
-    left = dp_of((x + NX - 1) % NX, yh, z)
-    other = 1 - yh
-
-    def to_sibling(i, ref):
-        put(ref, ref, sib_send.at[i], sib_recv.at[i], dp, ctx ^ 1)
-
-    put(piece(x, yh), piece(x, yh), by_send, by_recv, dp_of(x, other, z), ctx)
-    put(piece(x, yh), piece(x, yh), bx_send.at[0], bx_recv.at[0], right, ctx)
-    put(piece(x, yh), piece(x, yh), bx_send.at[1], bx_recv.at[1], left, ctx)
-    to_sibling(0, piece(x, yh))
-
-    settle(got_ref.at[pl.ds(1, n_dp - 1)], a_recv)
-    got = got_ref[...].astype(F32).reshape(n_dp * cap, width + tile)
-    slots = jnp.transpose(got[:, width:])[0:1]
-    lane = lax.broadcasted_iota(jnp.int32, (rows, n_dp * cap), 0).astype(F32) + 1.0
+    def send_pair():
+        settle(piece(x, other), by_recv)
+        put(piece(x, other), piece(x, other), bx_send.at[2], bx_recv.at[2], right, ctx)
+        put(piece(x, other), piece(x, other), bx_send.at[3], bx_recv.at[3], left, ctx)
+        to_sibling(1, piece(x, other))
+
+    send_pair()
+
+    settle(gmeta_ref.at[pl.ds(0, n_dp - 1)], m_recv)
+    spots = n_dp * cap
+    spot = lax.broadcasted_iota(jnp.int32, (tile, spots), 1)
+    spread = jnp.where(lax.broadcasted_iota(jnp.int32, (tile, spots), 0) == spot % cap, 1.0, 0.0).astype(BF)
+    spread = dot(gmeta_ref[...].reshape(n_dp, tile).astype(BF), spread)
+    spot = lax.broadcasted_iota(jnp.int32, (n_dp, spots), 1)
+    from_peer = lax.broadcasted_iota(jnp.int32, (n_dp, spots), 0) == spot // cap
+    slots = jnp.sum(jnp.where(from_peer, spread, 0.0), axis=0, keepdims=True)
+    lane = lax.broadcasted_iota(jnp.int32, (rows, spots), 0).astype(F32) + 1.0
     place = jnp.where(lane == slots, 1.0, 0.0).astype(BF)
-    placed = dot(place, got[:, :width].astype(BF))
+    settle(got_ref.at[pl.ds(0, n_dp - 1)], a_recv)
+    got = got_ref[...].astype(F32).reshape(spots, width).astype(BF)
+    placed = dot(place, got)
     placed_ref[...] = placed
-    normed = layer_norm(placed, again_ref[...]).astype(BF)
+    normed = layer_norm(placed, again_ref[...][None]).astype(BF)
 
     load_qkv.wait()
     base = pl.multiple_of(ctx * rows, rows)
@@ -241,65 +280,76 @@
         kv_ref[pl.ds(base, rows), 2 * g * group : (2 * g + 1) * group] = keys[:, g * group : (g + 1) * group]
         kv_ref[pl.ds(base, rows), (2 * g + 1) * group : (2 * g + 2) * group] = values[:, g * group : (g + 1) * group]
 
-    def kv_part(c, g):
-        return kv_ref.at[pl.ds(pl.multiple_of(c * rows, rows), rows), pl.ds(2 * g * group, 2 * group)]
-
-    for g in range(2):
-        part = kv_part(ctx, g)
-        put(part, part, kv_send.at[g, 0], kv_recv.at[g, 0], dp, ctx ^ 2)
-        put(part, part, kv_send.at[g, 1], kv_recv.at[g, 1], dp, ctx ^ 1)
+    def kv_part(c, i):
+        return kv_ref.at[pl.ds(pl.multiple_of(c * rows, rows), rows), pl.ds(i * group, group)]
+
+    for i in range(4):
+        part = kv_part(ctx, i)
+        put(part, part, kv_send.at[i, 0], kv_recv.at[i, 0], dp, ctx ^ 2)
+        put(part, part, kv_send.at[i, 1], kv_recv.at[i, 1], dp, ctx ^ 1)
     scale = math.log2(math.e) / math.sqrt(head)
     q_ref[...] = (dot(normed, wqkv_ref[:, :head_cols]) * scale).astype(BF)
 
-    settle(piece(x, other), by_recv)
-    put(piece(x, other), piece(x, other), bx_send.at[2], bx_recv.at[2], right, ctx)
-    put(piece(x, other), piece(x, other), bx_send.at[3], bx_recv.at[3], left, ctx)
-    to_sibling(1, piece(x, other))
-
-    def attend(g):
-        settle(kv_part(ctx ^ 2, g), kv_recv.at[g, 0])
-        part = kv_part(ctx ^ 2, g)
-        put(part, part, kv_send.at[g, 2], kv_recv.at[g, 2], dp, ctx ^ 1)
-        settle(part, kv_recv.at[g, 1])
-        settle(part, kv_recv.at[g, 2])
-        tiles = [None] * (group // tile)
+    def arrive(i):
+        part = kv_part(ctx ^ 2, i)
+        settle(part, kv_recv.at[i, 0])
+        put(part, part, kv_send.at[i, 2], kv_recv.at[i, 2], dp, ctx ^ 1)
+        settle(part, kv_recv.at[i, 1])
+        settle(part, kv_recv.at[i, 2])
+
+    def windows(h):
+        lo, hi = h * head, (h + 1) * head
+        c0, c1 = lo // tile * tile, (hi + tile - 1) // tile * tile
+        lanes = lax.broadcasted_iota(jnp.int32, (rows, c1 - c0), 1) + c0
+        return c0, c1, (lanes >= lo) & (lanes < hi)
+
+    def score(g):
+        totals = []
         for h in range(HEADS // 2):
-            lo, hi = h * head, (h + 1) * head
-            t0, t1 = lo // tile, (hi + tile - 1) // tile
-            c0, c1 = t0 * tile, t1 * tile
-            lanes = lax.broadcasted_iota(jnp.int32, (rows, c1 - c0), 1) + c0
-            inside = (lanes >= lo) & (lanes < hi)
+            c0, c1, inside = windows(h)
             query = q_ref[:, g * group + c0 : g * group + c1].astype(F32)
             query = jnp.where(inside, query, 0.0).astype(BF)
             scores = dot_nt(query, kv_ref[:, 2 * g * group + c0 : 2 * g * group + c1]) + bias_ref[...]
-            top = jnp.max(scores, axis=1, keepdims=True)
-            weights = jnp.exp2(scores - top)
-            total = jnp.sum(weights, axis=1, keepdims=True)
-            mixed = dot(weights.astype(BF), kv_ref[:, (2 * g + 1) * group + c0 : (2 * g + 1) * group + c1])
-            mixed = jnp.where(inside, mixed / total, 0.0)
-            for t in range(t0, t1):
-                term = mixed[:, (t - t0) * tile : (t - t0 + 1) * tile]
+            weights = jnp.exp2(scores - jnp.max(scores, axis=1, keepdims=True))
+            totals.append(jnp.sum(weights, axis=1, keepdims=True))
+            prob_ref[h] = weights.astype(BF)
+        return totals
+
+    def mix(g, totals):
+        tiles = [None] * (group // tile)
+        for h in range(HEADS // 2):
+            c0, c1, inside = windows(h)
+            mixed = dot(prob_ref[h], kv_ref[:, (2 * g + 1) * group + c0 : (2 * g + 1) * group + c1])
+            mixed = jnp.where(inside, mixed / totals[h], 0.0)
+            for t in range(c0 // tile, c1 // tile):
+                term = mixed[:, t * tile - c0 : (t + 1) * tile - c0]
                 tiles[t] = term if tiles[t] is None else tiles[t] + term
         for t, whole in enumerate(tiles):
             att_ref[:, g * group + t * tile : g * group + (t + 1) * tile] = whole.astype(BF)
 
-    attend(0)
+    arrive(0)
+    totals = score(0)
+    arrive(1)
+    mix(0, totals)
     settle(piece(x - 1, yh), bx_recv.at[0])
     settle(piece(x + 1, yh), bx_recv.at[1])
     put(piece(x - 1, yh), piece(x - 1, yh), bx_send.at[4], bx_recv.at[4], right, ctx)
     to_sibling(2, piece(x - 1, yh))
     to_sibling(3, piece(x + 1, yh))
-    attend(1)
+    arrive(2)
+    totals = score(1)
     settle(piece(x - 1, other), bx_recv.at[2])
     settle(piece(x + 1, other), bx_recv.at[3])
     put(piece(x + 1, other), piece(x + 1, other), bx_send.at[5], bx_recv.at[5], left, ctx)
     to_sibling(4, piece(x - 1, other))
     to_sibling(5, piece(x + 1, other))
+    arrive(3)
+    mix(1, totals)
 
     load_out.wait()
     after = (placed_ref[...] + dot(att_ref[...], wout_ref[...])).astype(BF)
     after_ref[...] = after
-    conv_normed = layer_norm(after.astype(F32), cgain_ref[...]).astype(BF)
+    conv_normed = layer_norm(after.astype(F32), cgain_ref[...][None]).astype(BF)
 
     settle(piece(x + 2, yh), bx_recv.at[4])
     to_sibling(6, piece(x + 2, yh))
@@ -345,7 +395,7 @@
                     k = 8 * a + b
                     term = shifted[8 * a : 8 * a + span] * mask_ref[k, r0 : r0 + span]
                     total = total + term * wdepth_ref[k : k + 1, lanes]
-            moved = total * bns_ref[:, lanes] + bnb_ref[:, lanes]
+            moved = total * bns_ref[lanes][None] + bnb_ref[lanes][None]
             act_ref[r0 : r0 + span, lanes] = (moved * jax.nn.sigmoid(moved)).astype(BF)
             return carry
 
@@ -372,7 +422,8 @@
     closing = closing + dot_nt(act_ref[:, quarter:], wfull_ref[1, :, channels:])
     out_ref[...] = (after_ref[...].astype(F32) + closing).astype(BF)
 
-    settle(send_ref.at[pl.ds(1, n_dp - 1)], a_send)
+    settle(send_ref.at[pl.ds(0, n_dp - 1)], a_send)
+    settle(meta_ref.at[pl.ds(0, n_dp - 1)], m_send)
     for k in range(1, nz):
         settle(zbuf_ref.at[0], bz_send.at[k])
     for d in range(1, 4):
@@ -382,9 +433,9 @@
         settle(piece(x, yh), bx_send.at[i])
     for i in range(NX * NY):
         settle(piece(x, yh), sib_send.at[i])
-    for g in range(2):
-        for i in range(3):
-            settle(kv_part(ctx, g), kv_send.at[g, i])
+    for i in range(4):
+        for j in range(3):
+            settle(kv_part(ctx, i), kv_send.at[i, j])
 
     @pl.when(ctx > 0)
     def _():
@@ -424,17 +475,6 @@
         shard_rows = w_pointin.shape[0]
         pad_rows = -(-shard_rows // 8) * 8
         half_cols = channels + channels // 2
-        flipped = w_pointout.T
-        shard = jnp.concatenate(
-            [
-                w_pointin[:, :channels],
-                flipped[:, : channels // 2],
-                w_pointin[:, channels:],
-                flipped[:, channels // 2 :],
-            ],
-            axis=1,
-        )
-        shard = jnp.pad(shard, ((0, pad_rows - shard_rows), (0, 0)))[None]
         pick = np.zeros((nz * n_ctx * shard_rows, n_ctx * nz * pad_rows), np.float32)
         for a in range(nz):
             for b in range(n_ctx):
@@ -453,13 +493,16 @@
             body,
             name="conformer_layer",
             out_shape=jax.ShapeDtypeStruct((rows, width), BF),
-            in_specs=[vmem, vmem, vmem, smem, vmem, hbm, hbm] + [vmem] * 6,
+            in_specs=[vmem, vmem, vmem, smem, vmem, hbm, hbm] + [vmem] * 7,
             out_specs=vmem,
             scratch_shapes=[
                 pltpu.VMEM(w_qkv.shape, BF),
                 pltpu.VMEM(w_out.shape, BF),
-                pltpu.VMEM((n_dp, cap, width + 128), BF),
-                pltpu.VMEM((n_dp, cap, width + 128), BF),
+                pltpu.VMEM((n_dp, cap, width), BF),
+                pltpu.VMEM((n_dp, cap, width), BF),
+                pltpu.VMEM((n_dp, 1, 128), F32),
+                pltpu.VMEM((n_dp, 1, 128), F32),
+                pltpu.VMEM((HEADS // 2, rows, seq), BF),
                 pltpu.VMEM((nz, pad_rows, 2 * half_cols), BF),
                 pltpu.VMEM((n_ctx, nz, pad_rows, half_cols), BF),
                 pltpu.VMEM((2, width, half_cols), BF),
@@ -480,6 +523,8 @@
                 dma((2,)),
                 dma,
                 dma,
+                dma,
+                dma,
                 dma((8,)),
                 dma((8,)),
                 dma((4,)),
@@ -490,8 +535,8 @@
                 dma((6,)),
                 dma((NX * NY,)),
                 dma((NX * NY,)),
-                dma((2, 3)),
-                dma((2, 3)),
+                dma((4, 3)),
+                dma((4, 3)),
                 dma((2,)),
                 dma((2,)),
             ],
@@ -504,16 +549,36 @@
             frames[0],
             segments,
             tile_mask[0],
-            attn_gain[None],
+            attn_gain,
             w_qkv,
             w_out,
-            conv_gain[None],
-            shard,
+            conv_gain,
+            w_pointin,
+            w_pointout.T,
             pick,
             w_depth,
-            bn_scale[None],
-            bn_shift[None],
+            bn_scale,
+            bn_shift,
         )
+
+        def hand_on(src_ref, dst_ref, sem):
+            copies = []
+            for i in range(4):
+                part = pl.ds(i * (rows // 4), rows // 4)
+                copies.append(pltpu.make_async_copy(src_ref.at[part], dst_ref.at[part], sem.at[i]))
+                copies[i].start()
+            for copy in copies:
+                copy.wait()
+
+        out = pl.pallas_call(
+            hand_on,
+            name="result",
+            out_shape=jax.ShapeDtypeStruct((rows, width), BF),
+            in_specs=[hbm],
+            out_specs=hbm,
+            scratch_shapes=[dma((4,))],
+            compiler_params=pltpu.CompilerParams(vmem_limit_bytes=2**20),
+        )(out)
         return out[None]
 
     return jax.shard_map(

time: 113 us -> 109 us (0.965)
  local copies, waits for them, and re-layouts: 8.63 us -> 1.13 us
  Pallas kernels: 104 us -> 108 us
    broadcast_in_dim x4 -> x0, local copies, waits for them, and re-layouts: 5.13 us -> none  [the longest x1 1.29 us: per_device(): attn_gain[None]]
    pallas_call x1, Pallas kernels: 104 us -> 107 us  [per_device(): pl.pallas_call(body, name='conformer_layer', out_shape=jax.ShapeDtypeStru...]
    slice x2 -> x0, local copies, waits for them, and re-layouts: 1.44 us -> none  [the longest x1 0.73 us: per_device(): w_pointin[:, :channels]]
where the time goes in v2:
time: 109 us
  Pallas kernels  108 us (99%)
  local copies, waits for them, and re-layouts  1.13 us (1%)
    pallas_call x1, Pallas kernels, per_device(): pl.pallas_call(body, name='conformer_layer', out_shape=jax.ShapeDtypeStru...  107 us

profile of v2, /device:TPU:1, one launch (start us, length us, event | category | flops | bytes accessed | tf_op | source)
XLA Modules:
  0.0 108.6 jit_solution(11658888501264388519)
XLA Ops:
  0.0 106.6 %conformer_layer.1.src_ref = bf16[256,1536]{1,0:T(8,128)(2,1)} custom-call(s32[1,256]{1,0:T(1,128)} %refs_0_.1, bf16[256,1536]{1,0:T(8,128)(2,1)} %bitcast.4, s32[1,1024]{1,0:T(1,128)} %refs_2_.1, s32[2,8]{1,0:T(2,128)} %bitcast.6, f32[1536]{0:T(1024)} %refs_4_.1, bf16[1536,2304]{1,0:T(8,128)(2,1)} %refs_5_.1, bf16[768,1536]{1,0:T(8,128)(2,1)} %refs_6_.1, ...), custom_call_target="tpu_custom_call" | custom-call | flops 6000000000 | bytes 20000000 | tf_op jit(solution)/shard_map/conformer_layer/pallas_call | solution.py:492
  106.6 0.0 copy-start
  106.6 1.1 %copy-done = bf16[256,1536]{1,0:T(8,128)(2,1)S(1)} copy-done((bf16[256,1536]{1,0:T(8,128)(2,1)S(1)}, bf16[256,1536]{1,0:T(8,128)(2,1)}, u32[]{:S(2)}) %copy-start) | copy-done | bytes 786456
  107.7 0.9 result.1
Async XLA Ops:
  106.6 1.1 %copy-start = (bf16[256,1536]{1,0:T(8,128)(2,1)S(1)}, bf16[256,1536]{1,0:T(8,128)(2,1)}, u32[]{:S(2)}) copy-start(bf16[256,1536]{1,0:T(8,128)(2,1)} %conformer_layer.1.src_ref) | copy-start | bytes 2359300

commit v3 on v2

--- a/solution.py
+++ b/solution.py
@@ -175,16 +175,56 @@
         put(meta_ref.at[i], gmeta_ref.at[i], m_send, m_recv, peer(i), ctx)
         return carry
 
-    def piece(px, py):
+    def piece(px, py, part):
         start = pl.multiple_of((((px + NX) % NX) * NY + py) * block, 16)
-        return wfull_ref.at[core, pl.ds(start, block)]
+        cols = pl.ds(0, channels) if part == 0 else pl.ds(channels, half_cols - channels)
+        return wfull_ref.at[core, pl.ds(start, block), cols]
 
     right = dp_of((x + 1) % NX, yh, z)
     left = dp_of((x + NX - 1) % NX, yh, z)
     other = 1 - yh
 
-    def to_sibling(i, ref):
-        put(ref, ref, sib_send.at[i], sib_recv.at[i], dp, ctx ^ 1)
+    def to_sibling(i, px, py, part):
+        ref = piece(px, py, part)
+        put(ref, ref, sib_send.at[part, i], sib_recv.at[part, i], dp, ctx ^ 1)
+
+    def to_x(i, px, py, part, d):
+        ref = piece(px, py, part)
+        put(ref, ref, bx_send.at[part, i], bx_recv.at[part, i], d, ctx)
+
+    def own_to_x(part):
+        to_x(0, x, yh, part, right)
+        to_x(1, x, yh, part, left)
+
+    def pair_to_x(part):
+        settle(piece(x, other, part), by_recv.at[part])
+        to_x(2, x, other, part, right)
+        to_x(3, x, other, part, left)
+        to_sibling(1, x, other, part)
+
+    def hand_right(part):
+        settle(piece(x - 1, yh, part), bx_recv.at[part, 0])
+        settle(piece(x + 1, yh, part), bx_recv.at[part, 1])
+        to_x(4, x - 1, yh, part, right)
+        to_sibling(2, x - 1, yh, part)
+        to_sibling(3, x + 1, yh, part)
+
+    def hand_left(part):
+        settle(piece(x - 1, other, part), bx_recv.at[part, 2])
+        settle(piece(x + 1, other, part), bx_recv.at[part, 3])
+        to_x(5, x + 1, other, part, left)
+        to_sibling(4, x - 1, other, part)
+        to_sibling(5, x + 1, other, part)
+
+    def two_away(part):
+        settle(piece(x + 2, yh, part), bx_recv.at[part, 4])
+        to_sibling(6, x + 2, yh, part)
+        settle(piece(x + 2, other, part), bx_recv.at[part, 5])
+        to_sibling(7, x + 2, other, part)
+
+    def from_sibling(part):
+        for i in range(NX * NY):
+            settle(piece(x, yh, part), sib_recv.at[part, i])
 
     zbuf_ref[pl.ds(z, 1)] = jnp.zeros((1,) + zbuf_ref.shape[1:], BF)
     for c in range(2):
@@ -203,17 +243,33 @@
     to_peer = jnp.where(lax.broadcasted_iota(jnp.int32, (n_dp, rows), 0) == rel, 1.0, 0.0).astype(BF)
     meta_ref[...] = dot(to_peer, at_rank).reshape(n_dp, 1, tile)
     pl.semaphore_wait(barrier, n_dp - 1 + 3)
+    def along_z(root, k):
+        shard = zbuf_ref.at[(root + nz) % nz]
+        put(shard, shard, bz_send.at[k], bz_recv.at[k], dp_of(x, yh, (root + k + nz) % nz), ctx)
+
+    if nz == 8:
+        along_z(z, 2)
+        along_z(z, 6)
+    else:
+        for k in range(1, nz):
+            along_z(z, k)
+    lax.fori_loop(0, n_dp // 16, ship, 0)
+    if nz == 8:
+        settle(zbuf_ref.at[0], bz_recv.at[2])
+        for k in (1, 3, 4):
+            along_z(z - 2, k)
+        settle(zbuf_ref.at[0], bz_recv.at[6])
+        for k in (5, 7):
+            along_z(z + 2, k)
+    lax.fori_loop(n_dp // 16, n_dp // 8, ship, 0)
+    pack(1)
     for k in range(1, nz):
-        put(zbuf_ref.at[z], zbuf_ref.at[z], bz_send.at[k], bz_recv.at[k], dp_of(x, yh, (z + k) % nz), ctx)
-    lax.fori_loop(0, per, ship, 0)
-    pack(1)
-
-    for k in range(1, nz):
-        settle(zbuf_ref.at[0], bz_recv.at[k])
+        if nz != 8 or k not in (2, 6):
+            settle(zbuf_ref.at[0], bz_recv.at[k])
     for d in range(1, 4):
         cols = pl.ds(pl.multiple_of(((ctx ^ d) % 2) * half_cols, 128), half_cols)
         put(zbuf_ref.at[:, :, cols], cbuf_ref.at[ctx], bc_send.at[d], bc_recv.at[d], dp, ctx ^ d)
-    lax.fori_loop(per, 2 * per, ship, 0)
+    lax.fori_loop(n_dp // 8, n_dp // 4, ship, 0)
     mine = pl.ds(pl.multiple_of(core * half_cols, 128), half_cols)
     cbuf_ref[pl.ds(ctx, 1)] = zbuf_ref[:, :, mine][None]
     pack(2)
@@ -223,11 +279,14 @@
     padded = cbuf_ref[...].astype(F32).reshape(pick_ref.shape[1], half_cols).astype(BF)
     own_start = pl.multiple_of((x * NY + yh) * block, 16)
     wfull_ref[core, pl.ds(own_start, block)] = dot(pick_ref[...], padded).astype(BF)
-    put(piece(x, yh), piece(x, yh), by_send, by_recv, dp_of(x, other, z), ctx)
-    put(piece(x, yh), piece(x, yh), bx_send.at[0], bx_recv.at[0], right, ctx)
-    put(piece(x, yh), piece(x, yh), bx_send.at[1], bx_recv.at[1], left, ctx)
-    to_sibling(0, piece(x, yh))
-    lax.fori_loop(2 * per, n_dp - 1, ship, 0)
+    for part in range(2):
+        ref = piece(x, yh, part)
+        put(ref, ref, by_send.at[part], by_recv.at[part], dp_of(x, other, z), ctx)
+        if part == 0:
+            own_to_x(0)
+        to_sibling(0, x, yh, part)
+    lax.fori_loop(per, n_dp - 1, ship, 0)
+    own_to_x(1)
     got_ref[n_dp - 1] = send_ref[n_dp - 1]
     gmeta_ref[n_dp - 1] = meta_ref[n_dp - 1]
 
@@ -248,13 +307,8 @@
     for k in range(taps):
         mask_ref[k] = jnp.where(segn_ref[k : k + rows] == own_seg, 1.0, 0.0)
 
-    def send_pair():
-        settle(piece(x, other), by_recv)
-        put(piece(x, other), piece(x, other), bx_send.at[2], bx_recv.at[2], right, ctx)
-        put(piece(x, other), piece(x, other), bx_send.at[3], bx_recv.at[3], left, ctx)
-        to_sibling(1, piece(x, other))
-
-    send_pair()
+    pair_to_x(0)
+    pair_to_x(1)
 
     settle(gmeta_ref.at[pl.ds(0, n_dp - 1)], m_recv)
     spots = n_dp * cap
@@ -327,22 +381,15 @@
         for t, whole in enumerate(tiles):
             att_ref[:, g * group + t * tile : g * group + (t + 1) * tile] = whole.astype(BF)
 
+    hand_right(0)
     arrive(0)
     totals = score(0)
+    hand_left(0)
     arrive(1)
     mix(0, totals)
-    settle(piece(x - 1, yh), bx_recv.at[0])
-    settle(piece(x + 1, yh), bx_recv.at[1])
-    put(piece(x - 1, yh), piece(x - 1, yh), bx_send.at[4], bx_recv.at[4], right, ctx)
-    to_sibling(2, piece(x - 1, yh))
-    to_sibling(3, piece(x + 1, yh))
     arrive(2)
     totals = score(1)
-    settle(piece(x - 1, other), bx_recv.at[2])
-    settle(piece(x + 1, other), bx_recv.at[3])
-    put(piece(x + 1, other), piece(x + 1, other), bx_send.at[5], bx_recv.at[5], left, ctx)
-    to_sibling(4, piece(x - 1, other))
-    to_sibling(5, piece(x + 1, other))
+    hand_right(1)
     arrive(3)
     mix(1, totals)
 
@@ -351,12 +398,9 @@
     after_ref[...] = after
     conv_normed = layer_norm(after.astype(F32), cgain_ref[...][None]).astype(BF)
 
-    settle(piece(x + 2, yh), bx_recv.at[4])
-    to_sibling(6, piece(x + 2, yh))
-    settle(piece(x + 2, other), bx_recv.at[5])
-    to_sibling(7, piece(x + 2, other))
-    for i in range(NX * NY):
-        settle(piece(x, yh), sib_recv.at[i])
+    two_away(0)
+    hand_left(1)
+    from_sibling(0)
 
     gate = jax.nn.sigmoid(dot(conv_normed, wfull_ref[1, :, :channels]))
     gated = (dot(conv_normed, wfull_ref[0, :, :channels]) * gate).astype(BF)
@@ -404,6 +448,8 @@
     for r0 in range(span, rows - span, span):
         convolve(r0)
 
+    two_away(1)
+
     @pl.when(ctx > 0)
     def _():
         settle(htop_ref, halo_recv.at[1])
@@ -417,6 +463,7 @@
     convolve(0)
     convolve(rows - span)
 
+    from_sibling(1)
     quarter = channels // 2
     closing = dot_nt(act_ref[:, :quarter], wfull_ref[0, :, channels:])
     closing = closing + dot_nt(act_ref[:, quarter:], wfull_ref[1, :, channels:])
@@ -428,11 +475,12 @@
         settle(zbuf_ref.at[0], bz_send.at[k])
     for d in range(1, 4):
         settle(cbuf_ref.at[0], bc_send.at[d])
-    settle(piece(x, yh), by_send)
-    for i in range(6):
-        settle(piece(x, yh), bx_send.at[i])
-    for i in range(NX * NY):
-        settle(piece(x, yh), sib_send.at[i])
+    for part in range(2):
+        settle(piece(x, yh, part), by_send.at[part])
+        for i in range(6):
+            settle(piece(x, yh, part), bx_send.at[part, i])
+        for i in range(NX * NY):
+            settle(piece(x, yh, part), sib_send.at[part, i])
     for i in range(4):
         for j in range(3):
             settle(kv_part(ctx, i), kv_send.at[i, j])
@@ -529,12 +577,12 @@
                 dma((8,)),
                 dma((4,)),
                 dma((4,)),
-                dma,
-                dma,
-                dma((6,)),
-                dma((6,)),
-                dma((NX * NY,)),
-                dma((NX * NY,)),
+                dma((2,)),
+                dma((2,)),
+                dma((2, 6)),
+                dma((2, 6)),
+                dma((2, NX * NY)),
+                dma((2, NX * NY)),
                 dma((4, 3)),
                 dma((4, 3)),
                 dma((2,)),
@@ -577,7 +625,7 @@
             in_specs=[hbm],
             out_specs=hbm,
             scratch_shapes=[dma((4,))],
-            compiler_params=pltpu.CompilerParams(vmem_limit_bytes=2**20),
+            compiler_params=pltpu.CompilerParams(vmem_limit_bytes=60 * 2**20),
         )(out)
         return out[None]
 

time: 109 us -> 122 us (1.12)
  Pallas kernels: 108 us -> 121 us
    pallas_call x1, Pallas kernels: 0.9 us -> 25 us  [per_device(): pl.pallas_call(hand_on, name='result', out_shape=jax.ShapeDtypeStruct((ro...]
    pallas_call x1, Pallas kernels: 107 us -> 96.2 us  [per_device(): pl.pallas_call(body, name='conformer_layer', out_shape=jax.ShapeDtypeStru...]
where the time goes in v3:
time: 122 us; the launch traced here: 121 us
  Pallas kernels  121 us (99%)
    pallas_call x1, Pallas kernels, per_device(): pl.pallas_call(body, name='conformer_layer', out_shape=jax.ShapeDtypeStru...  96.2 us
    pallas_call x1, Pallas kernels, per_device(): pl.pallas_call(hand_on, name='result', out_shape=jax.ShapeDtypeStruct((ro...  25 us

profile of v3, /device:TPU:1, one launch (start us, length us, event | category | flops | bytes accessed | tf_op | source)
XLA Modules:
  0.0 121.1 jit_solution(5918876739842509630)
XLA Ops:
  0.0 96.2 %conformer_layer.1.src_ref = bf16[256,1536]{1,0:T(8,128)(2,1)} custom-call(s32[1,256]{1,0:T(1,128)} %refs_0_.1, bf16[256,1536]{1,0:T(8,128)(2,1)} %bitcast.4, s32[1,1024]{1,0:T(1,128)} %refs_2_.1, s32[2,8]{1,0:T(2,128)} %bitcast.6, f32[1536]{0:T(1024)} %refs_4_.1, bf16[1536,2304]{1,0:T(8,128)(2,1)} %refs_5_.1, bf16[768,1536]{1,0:T(8,128)(2,1)} %refs_6_.1, ...), custom_call_target="tpu_custom_call" | custom-call | flops 6000000000 | bytes 20000000 | tf_op jit(solution)/shard_map/conformer_layer/pallas_call | solution.py:540
  96.2 25.0 %result.1 = bf16[256,1536]{1,0:T(8,128)(2,1)} custom-call(bf16[256,1536]{1,0:T(8,128)(2,1)} %conformer_layer.1.src_ref), custom_call_target="tpu_custom_call" | custom-call | tf_op jit(solution)/shard_map/result/pallas_call | solution.py:621

commit v4 on v3

--- a/solution.py
+++ b/solution.py
@@ -82,8 +82,6 @@
     m_recv,
     bz_send,
     bz_recv,
-    bc_send,
-    bc_recv,
     by_send,
     by_recv,
     bx_send,
@@ -102,7 +100,7 @@
     head_cols = wout_ref.shape[0]
     head = head_cols // HEADS
     group = head_cols // 2
-    half_cols = cbuf_ref.shape[3]
+    half_cols = cbuf_ref.shape[4]
     block = wfull_ref.shape[1] // (NX * NY)
     channels = wdepth_ref.shape[1]
     taps = wdepth_ref.shape[0]
@@ -142,6 +140,7 @@
     lax.fori_loop(0, n_dp - 1, greet, 0)
     for d in range(1, 4):
         pl.semaphore_signal(barrier, inc=1, device_id=(dp, ctx ^ d), device_id_type=MESH)
+        pl.semaphore_signal(barrier, inc=1, device_id=(dp_of(x, 1 - yh, z), ctx ^ d), device_id_type=MESH)
 
     load_qkv = pltpu.make_async_copy(wqkv_hbm, wqkv_ref, load_sem.at[0])
     load_qkv.start()
@@ -197,10 +196,8 @@
         to_x(1, x, yh, part, left)
 
     def pair_to_x(part):
-        settle(piece(x, other, part), by_recv.at[part])
         to_x(2, x, other, part, right)
         to_x(3, x, other, part, left)
-        to_sibling(1, x, other, part)
 
     def hand_right(part):
         settle(piece(x - 1, yh, part), bx_recv.at[part, 0])
@@ -242,51 +239,37 @@
     at_rank = jnp.where(rank_tall == lane, slot_tall, 0.0).astype(BF)
     to_peer = jnp.where(lax.broadcasted_iota(jnp.int32, (n_dp, rows), 0) == rel, 1.0, 0.0).astype(BF)
     meta_ref[...] = dot(to_peer, at_rank).reshape(n_dp, 1, tile)
-    pl.semaphore_wait(barrier, n_dp - 1 + 3)
-    def along_z(root, k):
-        shard = zbuf_ref.at[(root + nz) % nz]
-        put(shard, shard, bz_send.at[k], bz_recv.at[k], dp_of(x, yh, (root + k + nz) % nz), ctx)
-
-    if nz == 8:
-        along_z(z, 2)
-        along_z(z, 6)
-    else:
-        for k in range(1, nz):
-            along_z(z, k)
-    lax.fori_loop(0, n_dp // 16, ship, 0)
-    if nz == 8:
-        settle(zbuf_ref.at[0], bz_recv.at[2])
-        for k in (1, 3, 4):
-            along_z(z - 2, k)
-        settle(zbuf_ref.at[0], bz_recv.at[6])
-        for k in (5, 7):
-            along_z(z + 2, k)
-    lax.fori_loop(n_dp // 16, n_dp // 8, ship, 0)
+    pl.semaphore_wait(barrier, n_dp - 1 + 6)
+    for k in range(1, nz):
+        put(zbuf_ref.at[z], zbuf_ref.at[z], bz_send.at[k], bz_recv.at[k], dp_of(x, yh, (z + k) % nz), ctx)
+    lax.fori_loop(0, per, ship, 0)
     pack(1)
+    pack(2)
     for k in range(1, nz):
-        if nz != 8 or k not in (2, 6):
-            settle(zbuf_ref.at[0], bz_recv.at[k])
-    for d in range(1, 4):
+        settle(zbuf_ref.at[0], bz_recv.at[k])
+    for i in range(1, 2 * 4):
+        d, far = i // 2, i % 2
         cols = pl.ds(pl.multiple_of(((ctx ^ d) % 2) * half_cols, 128), half_cols)
-        put(zbuf_ref.at[:, :, cols], cbuf_ref.at[ctx], bc_send.at[d], bc_recv.at[d], dp, ctx ^ d)
-    lax.fori_loop(n_dp // 8, n_dp // 4, ship, 0)
+        to_yh = other if far else yh
+        put(zbuf_ref.at[:, :, cols], cbuf_ref.at[yh, ctx], by_send.at[i], by_recv.at[i], dp_of(x, to_yh, z), ctx ^ d)
+    lax.fori_loop(per, 3 * per, ship, 0)
     mine = pl.ds(pl.multiple_of(core * half_cols, 128), half_cols)
-    cbuf_ref[pl.ds(ctx, 1)] = zbuf_ref[:, :, mine][None]
-    pack(2)
+    cbuf_ref[yh, pl.ds(ctx, 1)] = zbuf_ref[:, :, mine][None]
     pack(3)
-    for d in range(1, 4):
-        settle(cbuf_ref.at[0], bc_recv.at[d])
-    padded = cbuf_ref[...].astype(F32).reshape(pick_ref.shape[1], half_cols).astype(BF)
-    own_start = pl.multiple_of((x * NY + yh) * block, 16)
-    wfull_ref[core, pl.ds(own_start, block)] = dot(pick_ref[...], padded).astype(BF)
+    for i in range(1, 2 * 4):
+        settle(cbuf_ref.at[0, 0], by_recv.at[i])
+    for y in range(NY):
+        padded = cbuf_ref[y].astype(F32).reshape(pick_ref.shape[1], half_cols).astype(BF)
+        start = pl.multiple_of((x * NY + y) * block, 16)
+        wfull_ref[core, pl.ds(start, block)] = dot(pick_ref[...], padded).astype(BF)
+    own_to_x(0)
+    pair_to_x(0)
+    lax.fori_loop(3 * per, n_dp - 1, ship, 0)
+    own_to_x(1)
+    pair_to_x(1)
     for part in range(2):
-        ref = piece(x, yh, part)
-        put(ref, ref, by_send.at[part], by_recv.at[part], dp_of(x, other, z), ctx)
-        if part == 0:
-            own_to_x(0)
         to_sibling(0, x, yh, part)
-    lax.fori_loop(per, n_dp - 1, ship, 0)
-    own_to_x(1)
+        to_sibling(1, x, other, part)
     got_ref[n_dp - 1] = send_ref[n_dp - 1]
     gmeta_ref[n_dp - 1] = meta_ref[n_dp - 1]
 
@@ -307,9 +290,6 @@
     for k in range(taps):
         mask_ref[k] = jnp.where(segn_ref[k : k + rows] == own_seg, 1.0, 0.0)
 
-    pair_to_x(0)
-    pair_to_x(1)
-
     settle(gmeta_ref.at[pl.ds(0, n_dp - 1)], m_recv)
     spots = n_dp * cap
     spot = lax.broadcasted_iota(jnp.int32, (tile, spots), 1)
@@ -473,10 +453,9 @@
     settle(meta_ref.at[pl.ds(0, n_dp - 1)], m_send)
     for k in range(1, nz):
         settle(zbuf_ref.at[0], bz_send.at[k])
-    for d in range(1, 4):
-        settle(cbuf_ref.at[0], bc_send.at[d])
+    for i in range(1, 2 * 4):
+        settle(cbuf_ref.at[0, 0], by_send.at[i])
     for part in range(2):
-        settle(piece(x, yh, part), by_send.at[part])
         for i in range(6):
             settle(piece(x, yh, part), bx_send.at[part, i])
         for i in range(NX * NY):
@@ -552,7 +531,7 @@
                 pltpu.VMEM((n_dp, 1, 128), F32),
                 pltpu.VMEM((HEADS // 2, rows, seq), BF),
                 pltpu.VMEM((nz, pad_rows, 2 * half_cols), BF),
-                pltpu.VMEM((n_ctx, nz, pad_rows, half_cols), BF),
+                pltpu.VMEM((NY, n_ctx, nz, pad_rows, half_cols), BF),
                 pltpu.VMEM((2, width, half_cols), BF),
                 pltpu.VMEM((seq, 2 * head_cols), BF),
                 pltpu.VMEM((rows, head_cols), BF),
@@ -575,10 +554,8 @@
                 dma,
                 dma((8,)),
                 dma((8,)),
-                dma((4,)),
-                dma((4,)),
-                dma((2,)),
-                dma((2,)),
+                dma((8,)),
+                dma((8,)),
                 dma((2, 6)),
                 dma((2, 6)),
                 dma((2, NX * NY)),
@@ -589,7 +566,7 @@
                 dma((2,)),
             ],
             compiler_params=pltpu.CompilerParams(
-                collective_id=0, has_side_effects=True, vmem_limit_bytes=60 * 2**20
+                collective_id=0, has_side_effects=True, vmem_limit_bytes=48 * 2**20
             ),
             cost_estimate=pl.CostEstimate(flops=6 * 10**9, bytes_accessed=20 * 10**6, transcendentals=3 * 10**6),
         )(
@@ -625,7 +602,7 @@
             in_specs=[hbm],
             out_specs=hbm,
             scratch_shapes=[dma((4,))],
-            compiler_params=pltpu.CompilerParams(vmem_limit_bytes=60 * 2**20),
+            compiler_params=pltpu.CompilerParams(vmem_limit_bytes=2**20),
         )(out)
         return out[None]
 

time: 122 us -> 117 us (0.959)
  Pallas kernels: 121 us -> 106 us
  local copies, waits for them, and re-layouts: 0 us -> 10.8 us
    pallas_call x1, Pallas kernels: 25 us -> 0.91 us  [per_device(): pl.pallas_call(hand_on, name='result', out_shape=jax.ShapeDtypeStruct((ro...]
    unnamed x0 -> x26, local copies, waits for them, and re-layouts: none -> 10.8 us
    pallas_call x1, Pallas kernels: 96.2 us -> 105 us  [per_device(): pl.pallas_call(body, name='conformer_layer', out_shape=jax.ShapeDtypeStru...]
where the time goes in v4:
time: 117 us
  Pallas kernels  106 us (91%)
  local copies, waits for them, and re-layouts  10.8 us (9%)
    pallas_call x1, Pallas kernels, per_device(): pl.pallas_call(body, name='conformer_layer', out_shape=jax.ShapeDtypeStru...  105 us
    unnamed x26, local copies, waits for them, and re-layouts  10.8 us

profile of v4, /device:TPU:1, one launch (start us, length us, event | category | flops | bytes accessed | tf_op | source)
XLA Modules:
  0.0 116.7 jit_solution(13582764749648274928)
XLA Ops:
  0.0 0.0 copy-start
  0.0 1.7 %copy-done = bf16[768,1536]{1,0:T(8,128)(2,1)S(1)} copy-done((bf16[768,1536]{1,0:T(8,128)(2,1)S(1)}, bf16[768,1536]{1,0:T(8,128)(2,1)}, u32[]{:S(2)}) %copy-start) | copy-done | bytes 2359320
  1.7 0.0 copy-start.1
  1.7 1.1 copy-done.1
  2.8 0.0 copy-start.2
  2.8 0.9 copy-done.2
  3.7 0.0 copy-start.3
  3.7 0.7 copy-done.3
  4.4 0.0 copy-start.4
  4.4 0.7 copy-done.4
  5.1 0.0 copy-start.5
  5.1 0.7 copy-done.5
  5.8 0.0 copy-start.6
  5.8 0.7 copy-done.6
  6.5 0.0 copy-start.7
  6.5 0.7 copy-done.7
  7.2 0.0 copy-start.8
  7.2 0.7 copy-done.8
  7.9 0.0 copy-start.9
  7.9 0.7 copy-done.9
  8.6 0.0 copy-start.10
  8.6 0.7 copy-done.10
  9.3 0.0 copy-start.11
  9.3 0.7 copy-done.11
  10.0 0.0 copy-start.12
  10.0 0.9 copy-done.12
  10.8 105.0 %conformer_layer.1.src_ref = bf16[256,1536]{1,0:T(8,128)(2,1)S(1)} custom-call(s32[1,256]{1,0:T(1,128)S(1)} %copy-done.10, bf16[256,1536]{1,0:T(8,128)(2,1)S(1)} %bitcast.4, s32[1,1024]{1,0:T(1,128)S(1)} %copy-done.7, s32[2,8]{1,0:T(2,128)S(1)} %bitcast.6, f32[1536]{0:T(1024)S(1)} %copy-done.5, bf16[1536,2304]{1,0:T(8,128)(2,1)} %refs_5_.1, ...), custom_call_target="tpu_custom_call" | custom-call | flops 6000000000 | bytes 20000000 | tf_op jit(solution)/shard_map/conformer_layer/pallas_call | solution.py:519
  115.8 0.9 result.1
Async XLA Ops:
  0.0 1.7 %copy-start = (bf16[768,1536]{1,0:T(8,128)(2,1)S(1)}, bf16[768,1536]{1,0:T(8,128)(2,1)}, u32[]{:S(2)}) copy-start(bf16[768,1536]{1,0:T(8,128)(2,1)} %refs_6_.1) | copy-start | bytes 7077892
  1.7 1.1 copy-start.1
  2.8 0.9 copy-start.2
  3.7 0.7 copy-start.3
  4.4 0.7 copy-start.4
  5.1 0.7 copy-start.5
  5.8 0.7 copy-start.6
  6.5 0.7 copy-start.7
  7.2 0.7 copy-start.8
  7.9 0.7 copy-start.9
  8.6 0.7 copy-start.10
  9.3 0.7 copy-start.11
  10.0 0.9 copy-start.12

commit v5 on v4

--- a/solution.py
+++ b/solution.py
@@ -36,6 +36,7 @@
 def layer_kernel(
     n_dp,
     shard_rows,
+    fetches,
     dest_ref,
     frames_ref,
     seg_ref,
@@ -147,6 +148,9 @@
     load_out = pltpu.make_async_copy(wout_hbm, wout_ref, load_sem.at[1])
     load_out.start()
 
+    for fetch in fetches:
+        fetch.wait()
+
     dest = dest_ref[...]
     owner = dest // rows
     slot = dest % rows
@@ -509,20 +513,48 @@
                     pick[(a * n_ctx + b) * shard_rows + j, (b * nz + a) * pad_rows + j] = 1.0
         pick = jnp.asarray(pick, BF)
         vmem = pl.BlockSpec(memory_space=pltpu.VMEM)
-        smem = pl.BlockSpec(memory_space=pltpu.SMEM)
-        hbm = pl.BlockSpec(memory_space=pl.ANY)
+        hbm = pl.BlockSpec(memory_space=pltpu.HBM)
+        operands = (
+            destinations,
+            frames[0],
+            segments,
+            tile_mask[0],
+            attn_gain,
+            w_qkv,
+            w_out,
+            conv_gain,
+            w_pointin,
+            w_pointout.T,
+            pick,
+            w_depth,
+            bn_scale,
+            bn_shift,
+        )
+        operands = tuple(pltpu.with_memory_space_constraint(a, pltpu.HBM) for a in operands)
+        fetched = [i for i in range(len(operands)) if i not in (5, 6)]
 
         def body(*refs):
-            layer_kernel(n_dp, shard_rows, *refs)
+            given, out_ref, rest = list(refs[: len(operands)]), refs[len(operands)], refs[len(operands) + 1 :]
+            local, sem, rest = rest[: len(fetched)], rest[len(fetched)], rest[len(fetched) + 1 :]
+            fetches = []
+            for j, i in enumerate(fetched):
+                fetches.append(pltpu.make_async_copy(given[i], local[j], sem.at[j]))
+                fetches[j].start()
+                given[i] = local[j]
+            layer_kernel(n_dp, shard_rows, fetches, *given, out_ref, *rest)
 
         dma = pltpu.SemaphoreType.DMA
         out = pl.pallas_call(
             body,
             name="conformer_layer",
             out_shape=jax.ShapeDtypeStruct((rows, width), BF),
-            in_specs=[vmem, vmem, vmem, smem, vmem, hbm, hbm] + [vmem] * 7,
+            in_specs=[hbm] * len(operands),
             out_specs=vmem,
             scratch_shapes=[
+                (pltpu.SMEM if i == 3 else pltpu.VMEM)(operands[i].shape, operands[i].dtype) for i in fetched
+            ]
+            + [
+                pltpu.SemaphoreType.DMA((len(fetched),)),
                 pltpu.VMEM(w_qkv.shape, BF),
                 pltpu.VMEM(w_out.shape, BF),
                 pltpu.VMEM((n_dp, cap, width), BF),
@@ -569,22 +601,7 @@
                 collective_id=0, has_side_effects=True, vmem_limit_bytes=48 * 2**20
             ),
             cost_estimate=pl.CostEstimate(flops=6 * 10**9, bytes_accessed=20 * 10**6, transcendentals=3 * 10**6),
-        )(
-            destinations,
-            frames[0],
-            segments,
-            tile_mask[0],
-            attn_gain,
-            w_qkv,
-            w_out,
-            conv_gain,
-            w_pointin,
-            w_pointout.T,
-            pick,
-            w_depth,
-            bn_scale,
-            bn_shift,
-        )
+        )(*operands)
 
         def hand_on(src_ref, dst_ref, sem):
             copies = []
@@ -599,8 +616,8 @@
             hand_on,
             name="result",
             out_shape=jax.ShapeDtypeStruct((rows, width), BF),
-            in_specs=[hbm],
-            out_specs=hbm,
+            in_specs=[pl.BlockSpec(memory_space=pl.ANY)],
+            out_specs=pl.BlockSpec(memory_space=pl.ANY),
             scratch_shapes=[dma((4,))],
             compiler_params=pltpu.CompilerParams(vmem_limit_bytes=2**20),
         )(out)

time: 117 us -> 106 us (0.906)
  local copies, waits for them, and re-layouts: 10.8 us -> 0 us
    unnamed x26 -> x0, local copies, waits for them, and re-layouts: 10.8 us -> none
where the time goes in v5:
time: 106 us; the launch traced here: 105 us
  Pallas kernels  105 us (99%)
    pallas_call x1, Pallas kernels, per_device(): pl.pallas_call(body, name='conformer_layer', out_shape=jax.ShapeDtypeStru...  105 us

profile of v5, /device:TPU:1, one launch (start us, length us, event | category | flops | bytes accessed | tf_op | source)
XLA Modules:
  0.0 105.5 jit_solution(16772893729948800707)
XLA Ops:
  0.0 104.6 %conformer_layer.1.src_ref = bf16[256,1536]{1,0:T(8,128)(2,1)S(1)} custom-call(s32[1,256]{1,0:T(1,128)} %refs_0_.1, bf16[256,1536]{1,0:T(8,128)(2,1)} %bitcast.4, s32[1,1024]{1,0:T(1,128)} %refs_2_.1, s32[2,8]{1,0:T(2,128)} %bitcast.6, f32[1536]{0:T(1024)} %refs_4_.1, bf16[1536,2304]{1,0:T(8,128)(2,1)} %refs_5_.1, bf16[768,1536]{1,0:T(8,128)(2,1)} %refs_6_.1, ...), custom_call_target="tpu_custom_call" | custom-call | flops 6000000000 | bytes 20000000 | tf_op jit(solution)/shard_map/conformer_layer/pallas_call | solution.py:547
  104.6 0.9 result.1

commit v6 on v5

--- a/solution.py
+++ b/solution.py
@@ -151,6 +151,19 @@
     for fetch in fetches:
         fetch.wait()
 
+    zbuf_ref[pl.ds(z, 1)] = jnp.zeros((1,) + zbuf_ref.shape[1:], BF)
+    for c in range(2):
+        left_col = c * half_cols
+        zbuf_ref[pl.ds(z, 1), :shard_rows, left_col : left_col + channels] = pin_ref[
+            :, c * channels : (c + 1) * channels
+        ][None]
+        zbuf_ref[pl.ds(z, 1), :shard_rows, left_col + channels : left_col + half_cols] = pout_ref[
+            :, c * (channels // 2) : (c + 1) * (channels // 2)
+        ][None]
+    pl.semaphore_wait(barrier, n_dp - 1 + 6)
+    for k in range(1, nz):
+        put(zbuf_ref.at[z], zbuf_ref.at[z], bz_send.at[k], bz_recv.at[k], dp_of(x, yh, (z + k) % nz), ctx)
+
     dest = dest_ref[...]
     owner = dest // rows
     slot = dest % rows
@@ -227,15 +240,6 @@
         for i in range(NX * NY):
             settle(piece(x, yh, part), sib_recv.at[part, i])
 
-    zbuf_ref[pl.ds(z, 1)] = jnp.zeros((1,) + zbuf_ref.shape[1:], BF)
-    for c in range(2):
-        left_col = c * half_cols
-        zbuf_ref[pl.ds(z, 1), :shard_rows, left_col : left_col + channels] = pin_ref[
-            :, c * channels : (c + 1) * channels
-        ][None]
-        zbuf_ref[pl.ds(z, 1), :shard_rows, left_col + channels : left_col + half_cols] = pout_ref[
-            :, c * (channels // 2) : (c + 1) * (channels // 2)
-        ][None]
     pack(0)
     rank_tall = jnp.transpose(jnp.broadcast_to(rank, (tile, rows)))
     slot_tall = jnp.transpose(jnp.broadcast_to(slot.astype(F32) + 1.0, (tile, rows)))
@@ -243,9 +247,6 @@
     at_rank = jnp.where(rank_tall == lane, slot_tall, 0.0).astype(BF)
     to_peer = jnp.where(lax.broadcasted_iota(jnp.int32, (n_dp, rows), 0) == rel, 1.0, 0.0).astype(BF)
     meta_ref[...] = dot(to_peer, at_rank).reshape(n_dp, 1, tile)
-    pl.semaphore_wait(barrier, n_dp - 1 + 6)
-    for k in range(1, nz):
-        put(zbuf_ref.at[z], zbuf_ref.at[z], bz_send.at[k], bz_recv.at[k], dp_of(x, yh, (z + k) % nz), ctx)
     lax.fori_loop(0, per, ship, 0)
     pack(1)
     pack(2)
@@ -269,8 +270,6 @@
     own_to_x(0)
     pair_to_x(0)
     lax.fori_loop(3 * per, n_dp - 1, ship, 0)
-    own_to_x(1)
-    pair_to_x(1)
     for part in range(2):
         to_sibling(0, x, yh, part)
         to_sibling(1, x, other, part)
@@ -366,14 +365,15 @@
             att_ref[:, g * group + t * tile : g * group + (t + 1) * tile] = whole.astype(BF)
 
     hand_right(0)
+    hand_left(0)
+    own_to_x(1)
+    pair_to_x(1)
     arrive(0)
     totals = score(0)
-    hand_left(0)
     arrive(1)
     mix(0, totals)
     arrive(2)
     totals = score(1)
-    hand_right(1)
     arrive(3)
     mix(1, totals)
 
@@ -383,7 +383,6 @@
     conv_normed = layer_norm(after.astype(F32), cgain_ref[...][None]).astype(BF)
 
     two_away(0)
-    hand_left(1)
     from_sibling(0)
 
     gate = jax.nn.sigmoid(dot(conv_normed, wfull_ref[1, :, :channels]))
@@ -429,6 +428,8 @@
 
         lax.fori_loop(0, channels // tile, body, 0)
 
+    hand_right(1)
+    hand_left(1)
     for r0 in range(span, rows - span, span):
         convolve(r0)
 

time: 106 us -> 108 us (1.019)
  Pallas kernels: 105 us -> 108 us
    pallas_call x1, Pallas kernels: 105 us -> 107 us  [per_device(): pl.pallas_call(body, name='conformer_layer', out_shape=jax.ShapeDtypeStru...]
where the time goes in v6:
time: 108 us
  Pallas kernels  108 us (100%)
    pallas_call x1, Pallas kernels, per_device(): pl.pallas_call(body, name='conformer_layer', out_shape=jax.ShapeDtypeStru...  107 us

profile of v6, /device:TPU:1, one launch (start us, length us, event | category | flops | bytes accessed | tf_op | source)
XLA Modules:
  0.0 107.8 jit_solution(15537327549370173086)
XLA Ops:
  0.0 106.9 %conformer_layer.1.src_ref = bf16[256,1536]{1,0:T(8,128)(2,1)S(1)} custom-call(s32[1,256]{1,0:T(1,128)} %refs_0_.1, bf16[256,1536]{1,0:T(8,128)(2,1)} %bitcast.4, s32[1,1024]{1,0:T(1,128)} %refs_2_.1, s32[2,8]{1,0:T(2,128)} %bitcast.6, f32[1536]{0:T(1024)} %refs_4_.1, bf16[1536,2304]{1,0:T(8,128)(2,1)} %refs_5_.1, bf16[768,1536]{1,0:T(8,128)(2,1)} %refs_6_.1, ...), custom_call_target="tpu_custom_call" | custom-call | flops 6000000000 | bytes 20000000 | tf_op jit(solution)/shard_map/conformer_layer/pallas_call | solution.py:548
  106.9 0.9 result.1

commit v7 on v6

--- a/solution.py
+++ b/solution.py
@@ -240,16 +240,16 @@
         for i in range(NX * NY):
             settle(piece(x, yh, part), sib_recv.at[part, i])
 
-    pack(0)
+    pack(3)
     rank_tall = jnp.transpose(jnp.broadcast_to(rank, (tile, rows)))
     slot_tall = jnp.transpose(jnp.broadcast_to(slot.astype(F32) + 1.0, (tile, rows)))
     lane = lax.broadcasted_iota(jnp.int32, (rows, tile), 1).astype(F32)
     at_rank = jnp.where(rank_tall == lane, slot_tall, 0.0).astype(BF)
     to_peer = jnp.where(lax.broadcasted_iota(jnp.int32, (n_dp, rows), 0) == rel, 1.0, 0.0).astype(BF)
     meta_ref[...] = dot(to_peer, at_rank).reshape(n_dp, 1, tile)
-    lax.fori_loop(0, per, ship, 0)
+    lax.fori_loop(3 * per, n_dp - 1, ship, 0)
+    pack(0)
     pack(1)
-    pack(2)
     for k in range(1, nz):
         settle(zbuf_ref.at[0], bz_recv.at[k])
     for i in range(1, 2 * 4):
@@ -257,10 +257,11 @@
         cols = pl.ds(pl.multiple_of(((ctx ^ d) % 2) * half_cols, 128), half_cols)
         to_yh = other if far else yh
         put(zbuf_ref.at[:, :, cols], cbuf_ref.at[yh, ctx], by_send.at[i], by_recv.at[i], dp_of(x, to_yh, z), ctx ^ d)
-    lax.fori_loop(per, 3 * per, ship, 0)
+    lax.fori_loop(0, 3 * n_dp // 8, ship, 0)
     mine = pl.ds(pl.multiple_of(core * half_cols, 128), half_cols)
     cbuf_ref[yh, pl.ds(ctx, 1)] = zbuf_ref[:, :, mine][None]
-    pack(3)
+    pack(2)
+    lax.fori_loop(3 * n_dp // 8, 3 * per, ship, 0)
     for i in range(1, 2 * 4):
         settle(cbuf_ref.at[0, 0], by_recv.at[i])
     for y in range(NY):
@@ -269,7 +270,8 @@
         wfull_ref[core, pl.ds(start, block)] = dot(pick_ref[...], padded).astype(BF)
     own_to_x(0)
     pair_to_x(0)
-    lax.fori_loop(3 * per, n_dp - 1, ship, 0)
+    own_to_x(1)
+    pair_to_x(1)
     for part in range(2):
         to_sibling(0, x, yh, part)
         to_sibling(1, x, other, part)
@@ -366,12 +368,12 @@
 
     hand_right(0)
     hand_left(0)
-    own_to_x(1)
-    pair_to_x(1)
     arrive(0)
     totals = score(0)
     arrive(1)
     mix(0, totals)
+    hand_right(1)
+    hand_left(1)
     arrive(2)
     totals = score(1)
     arrive(3)
@@ -428,8 +430,6 @@
 
         lax.fori_loop(0, channels // tile, body, 0)
 
-    hand_right(1)
-    hand_left(1)
     for r0 in range(span, rows - span, span):
         convolve(r0)
 

time: 108 us -> 93.6 us (0.87)
  Pallas kernels: 108 us -> 93.6 us
    pallas_call x1, Pallas kernels: 107 us -> 92.6 us  [per_device(): pl.pallas_call(body, name='conformer_layer', out_shape=jax.ShapeDtypeStru...]
where the time goes in v7:
time: 93.6 us
  Pallas kernels  93.6 us (100%)
    pallas_call x1, Pallas kernels, per_device(): pl.pallas_call(body, name='conformer_layer', out_shape=jax.ShapeDtypeStru...  92.6 us

profile of v7, /device:TPU:1, one launch (start us, length us, event | category | flops | bytes accessed | tf_op | source)
XLA Modules:
  0.0 93.6 jit_solution(10674593750421247388)
XLA Ops:
  0.0 92.6 %conformer_layer.1.src_ref = bf16[256,1536]{1,0:T(8,128)(2,1)S(1)} custom-call(s32[1,256]{1,0:T(1,128)} %refs_0_.1, bf16[256,1536]{1,0:T(8,128)(2,1)} %bitcast.4, s32[1,1024]{1,0:T(1,128)} %refs_2_.1, s32[2,8]{1,0:T(2,128)} %bitcast.6, f32[1536]{0:T(1024)} %refs_4_.1, bf16[1536,2304]{1,0:T(8,128)(2,1)} %refs_5_.1, bf16[768,1536]{1,0:T(8,128)(2,1)} %refs_6_.1, ...), custom_call_target="tpu_custom_call" | custom-call | flops 6000000000 | bytes 20000000 | tf_op jit(solution)/shard_map/conformer_layer/pallas_call | solution.py:548
  92.7 0.9 result.1

commit v8 on v7

--- a/solution.py
+++ b/solution.py
@@ -366,10 +366,10 @@
         for t, whole in enumerate(tiles):
             att_ref[:, g * group + t * tile : g * group + (t + 1) * tile] = whole.astype(BF)
 
+    arrive(0)
+    totals = score(0)
     hand_right(0)
     hand_left(0)
-    arrive(0)
-    totals = score(0)
     arrive(1)
     mix(0, totals)
     hand_right(1)
@@ -385,10 +385,10 @@
     conv_normed = layer_norm(after.astype(F32), cgain_ref[...][None]).astype(BF)
 
     two_away(0)
+    near = dot(conv_normed, wfull_ref[core, :, :channels])
     from_sibling(0)
-
-    gate = jax.nn.sigmoid(dot(conv_normed, wfull_ref[1, :, :channels]))
-    gated = (dot(conv_normed, wfull_ref[0, :, :channels]) * gate).astype(BF)
+    far = dot(conv_normed, wfull_ref[1 - core, :, :channels])
+    gated = (jnp.where(core == 0, near, far) * jax.nn.sigmoid(jnp.where(core == 0, far, near))).astype(BF)
     gat_ref[...] = gated
     gf_ref[half : half + rows] = gated.astype(F32)
 
@@ -448,10 +448,15 @@
     convolve(0)
     convolve(rows - span)
 
+    quarter = channels // 2
+
+    def close(c):
+        lanes = pl.ds(pl.multiple_of(c * quarter, 128), quarter)
+        return dot_nt(act_ref[:, lanes], wfull_ref[c, :, channels:])
+
+    closing = close(core)
     from_sibling(1)
-    quarter = channels // 2
-    closing = dot_nt(act_ref[:, :quarter], wfull_ref[0, :, channels:])
-    closing = closing + dot_nt(act_ref[:, quarter:], wfull_ref[1, :, channels:])
+    closing = closing + close(1 - core)
     out_ref[...] = (after_ref[...].astype(F32) + closing).astype(BF)
 
     settle(send_ref.at[pl.ds(0, n_dp - 1)], a_send)

time: 93.6 us -> 93.4 us (level)
  no operation moved by 1% of the time
where the time goes in v8:
time: 93.4 us; the launch traced here: 93.3 us
  Pallas kernels  93.3 us (100%)
    pallas_call x1, Pallas kernels, per_device(): pl.pallas_call(body, name='conformer_layer', out_shape=jax.ShapeDtypeStru...  92.4 us

profile of v8, /device:TPU:1, one launch (start us, length us, event | category | flops | bytes accessed | tf_op | source)
XLA Modules:
  0.0 93.3 jit_solution(5040312015133460180)
XLA Ops:
  0.0 92.4 %conformer_layer.1.src_ref = bf16[256,1536]{1,0:T(8,128)(2,1)S(1)} custom-call(s32[1,256]{1,0:T(1,128)} %refs_0_.1, bf16[256,1536]{1,0:T(8,128)(2,1)} %bitcast.4, s32[1,1024]{1,0:T(1,128)} %refs_2_.1, s32[2,8]{1,0:T(2,128)} %bitcast.6, f32[1536]{0:T(1024)} %refs_4_.1, bf16[1536,2304]{1,0:T(8,128)(2,1)} %refs_5_.1, bf16[768,1536]{1,0:T(8,128)(2,1)} %refs_6_.1, ...), custom_call_target="tpu_custom_call" | custom-call | flops 6000000000 | bytes 20000000 | tf_op jit(solution)/shard_map/conformer_layer/pallas_call | solution.py:553
  92.4 0.9 result.1

commit v9 on v8

--- a/solution.py
+++ b/solution.py
@@ -372,10 +372,10 @@
     hand_left(0)
     arrive(1)
     mix(0, totals)
+    arrive(2)
+    totals = score(1)
     hand_right(1)
     hand_left(1)
-    arrive(2)
-    totals = score(1)
     arrive(3)
     mix(1, totals)
 

time: 93.4 us -> 93.4 us (level)
  no operation moved by 1% of the time
where the time goes in v9:
time: 93.4 us
  Pallas kernels  93.4 us (100%)
    pallas_call x1, Pallas kernels, per_device(): pl.pallas_call(body, name='conformer_layer', out_shape=jax.ShapeDtypeStru...  92.4 us

profile of v9, /device:TPU:1, one launch (start us, length us, event | category | flops | bytes accessed | tf_op | source)
XLA Modules:
  0.0 93.4 jit_solution(15528130014076960431)
XLA Ops:
  0.0 92.4 %conformer_layer.1.src_ref = bf16[256,1536]{1,0:T(8,128)(2,1)S(1)} custom-call(s32[1,256]{1,0:T(1,128)} %refs_0_.1, bf16[256,1536]{1,0:T(8,128)(2,1)} %bitcast.4, s32[1,1024]{1,0:T(1,128)} %refs_2_.1, s32[2,8]{1,0:T(2,128)} %bitcast.6, f32[1536]{0:T(1024)} %refs_4_.1, bf16[1536,2304]{1,0:T(8,128)(2,1)} %refs_5_.1, bf16[768,1536]{1,0:T(8,128)(2,1)} %refs_6_.1, ...), custom_call_target="tpu_custom_call" | custom-call | flops 6000000000 | bytes 20000000 | tf_op jit(solution)/shard_map/conformer_layer/pallas_call | solution.py:553
  92.5 0.9 result.1
